TPU v7x, 256 devices: a whole 4x4x8 slice. The times are simulated.
256 devices in a mesh: tensor: 8 (over y, core), expert: 8 (over x, z_hi), dp: 4 (over z_lo).
Axes of the slice: x: 4, y: 4, z: 8 (z_hi: 2, z_lo: 4; z = z_hi * 4 + z_lo), core: 2. Of those that a mesh axis runs over, the one named last changes fastest.
Arguments:
- tokens: bfloat16 [4096, 3072], P(('expert', 'dp'), 'tensor'), may hold values from -6 to 6
- routes: int32 [4096, 2], P(('expert', 'dp')), may hold values from 0 to 7, all different within a row; in each aligned block of 128 rows (0 to 127, 128 to 255, ...) at most 64 rows name the same one
- up_weight: bfloat16 [8, 3072, 16384], P('expert', 'dp', 'tensor'), may hold values from -0.109375 to 0.109375
- saved_pre: bfloat16 [8, 2048, 16384], P('expert', 'dp', 'tensor'), may hold values from -6 to 6
- grad_act: bfloat16 [8, 2048, 16384], P('expert', 'dp', 'tensor'), may hold values from -1.5 to 1.5
Outputs:
- token_grad: bfloat16 [4096, 3072], P(('expert', 'dp'), 'tensor')
- up_grad: bfloat16 [8, 3072, 16384], P('expert', 'dp', 'tensor')
Inputs may be any that keep to these rules, and one draw needn't show every extreme that they name: `routes`: the two experts of a token differ. Among the 128 tokens of one source group no expert is named by more than 64 tokens.
All inputs are finite; a program needn't handle non-finite values.
Results may differ from a plain program's by a relative error of at most 0.02.
Values may be sent and summed in bfloat16 or wider, within the bound.
No kernel may reach another device: no remote copies, remote signals or barrier semaphores. Data moves between devices by JAX's collectives and lax.ppermute only.
A program may use at most 128 MiB of HBM per device.

v0:
```python
import jax
import jax.numpy as jnp
from jax import lax
from jax.sharding import PartitionSpec as P

root_coef = 0.7978845608028654
cubic_coef = 0.044715


def gelu_slope(pre_act):
    inner_arg = root_coef * (pre_act + cubic_coef * pre_act * pre_act * pre_act)
    tangent = jnp.tanh(inner_arg)
    return 0.5 * (1.0 + tangent) + 0.5 * pre_act * (1.0 - tangent * tangent) * root_coef * (
        1.0 + 3.0 * cubic_coef * pre_act * pre_act
    )


def place_slots(route_block, experts, capacity):
    tok_count = route_block.shape[0]
    ordered = jnp.transpose(route_block).reshape(-1)
    onehot = (ordered[:, None] == jnp.arange(experts, dtype=jnp.int32)[None, :]).astype(jnp.int32)
    before = jnp.cumsum(onehot, axis=0) - onehot
    position = jnp.sum(before * onehot, axis=1)
    return jnp.transpose((ordered * capacity + position).reshape(2, tok_count))


def per_device(tokens, routes, up_weight, saved_pre, grad_act):
    experts = lax.axis_size("expert")
    slot_count = saved_pre.shape[1]
    capacity = slot_count // experts
    tok_dev = tokens.shape[0]
    slot_index = place_slots(routes, experts, capacity)
    token_ids = jnp.broadcast_to(
        jnp.arange(tok_dev, dtype=jnp.int32)[:, None], (tok_dev, 2)
    ).reshape(-1)
    holder = jnp.zeros((slot_count,), jnp.int32).at[slot_index.reshape(-1)].set(token_ids + 1)
    filled = holder > 0
    source_row = jnp.maximum(holder - 1, 0)
    nothing = jnp.zeros((), jnp.bfloat16)
    gathered = lax.all_gather(tokens, "tensor", axis=1, tiled=True)
    outgoing = jnp.where(filled[:, None], jnp.take(gathered, source_row, axis=0), nothing)
    arrived = lax.all_to_all(outgoing, "expert", split_axis=0, concat_axis=0, tiled=True)
    unit_grad = (
        grad_act[0].astype(jnp.float32) * gelu_slope(saved_pre[0].astype(jnp.float32))
    ).astype(jnp.bfloat16)
    weight = up_weight[0]
    partial_sum = lax.dot_general(
        unit_grad,
        lax.all_gather(weight, "dp", axis=0, tiled=True),
        (((1,), (1,)), ((), ())),
        preferred_element_type=jnp.float32,
    )
    grad_block = lax.psum_scatter(
        lax.dot_general(
            arrived, unit_grad, (((0,), (0,)), ((), ())), preferred_element_type=jnp.float32
        ).astype(jnp.bfloat16),
        "dp",
        scatter_dimension=0,
        tiled=True,
    )
    summed = lax.psum_scatter(
        partial_sum.astype(jnp.bfloat16), "tensor", scatter_dimension=1, tiled=True
    )
    returned = lax.all_to_all(summed, "expert", split_axis=0, concat_axis=0, tiled=True)
    first_part = jnp.take(returned, slot_index[:, 0], axis=0).astype(jnp.float32)
    second = jnp.take(returned, slot_index[:, 1], axis=0).astype(jnp.float32)
    token_grad = (first_part + second).astype(jnp.bfloat16)
    return (token_grad, grad_block[None])


def solution(mesh):
    placed = (
        P(("expert", "dp"), "tensor"),
        P(("expert", "dp"), None),
        P("expert", "dp", "tensor"),
        P("expert", "dp", "tensor"),
        P("expert", "dp", "tensor"),
    )
    return jax.shard_map(
        per_device,
        mesh=mesh,
        in_specs=placed,
        out_specs=(P(("expert", "dp"), "tensor"), P("expert", "dp", "tensor")),
        check_vma=False,
    )
```

profile of v0, /device:TPU:166, one launch (start us, length us, event | category | flops | bytes accessed | tf_op | source)
XLA Modules:
  0.0 586.3 jit_solution(17833725543899326443)
XLA Ops:
  7.2 0.0 all-gather.3.cloned.1.call-start
  7.2 0.7 all-gather.3.cloned.1.call-update
  7.9 0.7 fusion.43
  8.6 0.6 reduce-window.6
  9.2 0.2 slice_reduce_fusion
  9.4 0.8 fusion.42
  10.2 0.7 fusion.44
  10.9 0.1 copy.8
  11.0 0.1 reshape.90
  11.1 0.1 reshape.121
  11.3 1.4 scatter_custom_fusion
  12.7 0.1 broadcast_in_dim.50
  12.8 0.1 broadcast_in_dim.52
  12.9 14.3 %all_gather.7 = bf16[128,3072]{1,0:T(8,128)(2,1)S(1)} all-gather(bf16[128,384]{1,0:T(8,128)(2,1)} %param.7), channel_id=1, replica_groups=mesh['tensor'=8,'expert'=8,'dp'=4] {'tensor'}, dimensions={1}, use_global_device_ids=true | all-gather | bytes 884736 | tf_op jit(solution)/shard_map/all_gather | solution.py:40
  27.2 3.8 gather_fusion
  31.0 4.3 select_select_fusion
  35.3 9.6 %all-to-all-start.1 = ((bf16[8,64,3072]{2,1,0:T(8,128)(2,1)}), bf16[8,64,3072]{2,1,0:T(8,128)(2,1)S(1)}, u32[]{:S(2)}, u32[]{:S(2)}) async-start(bf16[8,64,3072]{2,1,0:T(8,128)(2,1)} %select_select_fusion), calls=%async_computation.1 | async-start | bytes 6291456 | tf_op jit(solution)/shard_map/all_to_all | solution.py:42
  44.9 0.0 reduce-scatter.7.cloned.1.call-start
  44.9 253.1 %all-gather.3.cloned.1.call-done = bf16[1,3072,2048]{2,1,0:T(8,128)(2,1)} async-done(((bf16[1,768,2048]{2,1,0:T(8,128)(2,1)}), bf16[1,3072,2048]{2,1,0:T(8,128)(2,1)}) %all-gather.3.cloned.1.call-update) | async-done | bytes 12582928 | tf_op jit(solution)/shard_map/all_gather | solution.py:49
  298.0 15.2 %fusion.9 = bf16[512,3072]{1,0:T(8,128)(2,1)} fusion(bf16[1,3072,2048]{2,1,0:T(8,128)(2,1)} %all-gather.3.cloned.1.call-done, bf16[1,512,2048]{2,1,0:T(8,128)(2,1)} %param.11, bf16[1,512,2048]{2,1,0:T(8,128)(2,1)} %param.10), kind=kOutput, calls=%fused_computation.24 | convolution fusion | flops 6466043904 | bytes 19922944 | tf_op jit(solution)/shard_map/dot_general | solution.py:47
  313.2 4.7 copy.9
  317.9 0.0 reduce-scatter.7.cloned.1.call-update
  317.9 0.2 reduce-scatter.5.cloned.1.call-start
  318.2 0.0 all-to-all-done.1
  318.2 13.8 %convolution_convert_fusion = bf16[3072,2048]{1,0:T(8,128)(2,1)} fusion(bf16[512,3072]{1,0:T(8,128)(2,1)S(1)} %bitcast.98, bf16[1,512,2048]{2,1,0:T(8,128)(2,1)} %param.11, bf16[1,512,2048]{2,1,0:T(8,128)(2,1)} %param.10), kind=kOutput, calls=%fused_computation.14 | convolution fusion | flops 6470762496 | bytes 19922944 | tf_op jit(solution)/shard_map/dot_general | solution.py:54
  332.0 0.0 reduce-scatter.5.cloned.1.call-update
  332.0 25.8 %reduce-scatter.7.cloned.1.call-done = bf16[384,512]{1,0:T(8,128)(2,1)} async-done(((bf16[3072,512]{1,0:T(8,128)(2,1)}), bf16[384,512]{1,0:T(8,128)(2,1)}) %reduce-scatter.7.cloned.1.call-update) | async-done | bytes 393232
  357.8 1.9 copy.10
  359.8 9.6 %all-to-all-start = ((bf16[8,64,384]{2,1,0:T(8,128)(2,1)}), bf16[8,64,384]{2,1,0:T(8,128)(2,1)S(1)}, u32[]{:S(2)}, u32[]{:S(2)}) async-start(bf16[8,64,384]{2,1,0:T(8,128)(2,1)} %bitcast.10), calls=%async_computation | async-start | bytes 786432 | tf_op jit(solution)/shard_map/all_to_all | solution.py:64
  369.4 13.9 %all-to-all-done = bf16[8,64,384]{2,1,0:T(8,128)(2,1)S(1)} async-done(((bf16[8,64,384]{2,1,0:T(8,128)(2,1)}), bf16[8,64,384]{2,1,0:T(8,128)(2,1)S(1)}, u32[]{:S(2)}, u32[]{:S(2)}) %all-to-all-start) | async-done | bytes 393248 | tf_op jit(solution)/shard_map/all_to_all | solution.py:64
  383.3 0.9 gather_fusion.2
  384.2 0.9 gather_fusion.1
  385.1 0.8 add_convert_fusion
  385.8 194.0 %reduce-scatter.5.cloned.1.call-done = bf16[768,2048]{1,0:T(8,128)(2,1)} async-done(((bf16[3072,2048]{1,0:T(8,128)(2,1)}), bf16[768,2048]{1,0:T(8,128)(2,1)}) %reduce-scatter.5.cloned.1.call-update) | async-done | bytes 3145744 | tf_op jit(solution)/shard_map/reduce_scatter | solution.py:53
  (9 shorter events, 0.1 us)
Async XLA Ops:
  7.2 290.8 %all-gather.3.cloned.1.call-start = ((), (), s32[]{:S(2)}) async-start(), calls=%async_computation.5 | async-start | bytes 15728640 | tf_op jit(solution)/shard_map/all_gather | solution.py:49
  35.3 282.9 %all-to-all-start.1 = ((bf16[8,64,3072]{2,1,0:T(8,128)(2,1)}), bf16[8,64,3072]{2,1,0:T(8,128)(2,1)S(1)}, u32[]{:S(2)}, u32[]{:S(2)}) async-start(bf16[8,64,3072]{2,1,0:T(8,128)(2,1)} %select_select_fusion), calls=%async_computation.1 | async-start | bytes 6291456 | tf_op jit(solution)/shard_map/all_to_all | solution.py:42
  44.9 313.0 %reduce-scatter.7.cloned.1.call-start = ((), (), s32[]{:S(2)}) async-start(), calls=%async_computation.6 | async-start | bytes 3538944
  317.9 261.8 %reduce-scatter.5.cloned.1.call-start = ((), (), s32[]{:S(2)}) async-start(), calls=%async_computation.4 | async-start | bytes 15728640 | tf_op jit(solution)/shard_map/reduce_scatter | solution.py:53
  359.8 23.6 %all-to-all-start = ((bf16[8,64,384]{2,1,0:T(8,128)(2,1)}), bf16[8,64,384]{2,1,0:T(8,128)(2,1)S(1)}, u32[]{:S(2)}, u32[]{:S(2)}) async-start(bf16[8,64,384]{2,1,0:T(8,128)(2,1)} %bitcast.10), calls=%async_computation | async-start | bytes 786432 | tf_op jit(solution)/shard_map/all_to_all | solution.py:64
Sparse Core Ops, SparseCore 0:
  9.8 288.1 all-gather.2
  318.1 39.7 reduce-scatter.6
  361.0 218.7 reduce-scatter.4
where the time goes:
time: 591 us; the launch traced here: 586 us
  waiting for transfers between devices  488 us (83%)
  matrix products  29 us (5%)
  starting transfers between devices  19.5 us (3%)
  local copies, waits for them, and re-layouts  14.4 us (2%)
  blocking collectives  14.3 us (2%)
  between operations  13.8 us (2%)
  other arithmetic  7.82 us (1%)
    all_gather x1, waiting for transfers between devices, per_device(): lax.all_gather(weight, 'dp', axis=0, tiled=True)  253 us
    reduce_scatter x1, waiting for transfers between devices, per_device(): lax.psum_scatter(lax.dot_general(arrived, unit_grad, (((0,), (0,)), ((),...  194 us
    unnamed x4, waiting for transfers between devices  26.5 us
    dot_general x1, matrix products, per_device(): lax.dot_general(unit_grad, lax.all_gather(weight, 'dp', axis=0, tiled=Tru...  15.2 us
    all_gather x1, blocking collectives, per_device(): gathered = lax.all_gather(tokens, 'tensor', axis=1, tiled=True)  14.3 us
    all_to_all x1, waiting for transfers between devices, per_device(): lax.all_to_all(summed, 'expert', split_axis=0, concat_axis=0, tiled=True)  13.9 us
    dot_general x1, matrix products, per_device(): lax.dot_general(arrived, unit_grad, (((0,), (0,)), ((), ())), preferred_e...  13.8 us
  transfers between devices with their start and end apart: 5, of which 4 were waited for; matrix products, arithmetic and copies ran while one was open for 9% of the time, Pallas kernels for 0%

commit v1 on v0

v1 whole, which is shorter than its diff:
```python
import jax
import jax.numpy as jnp
from jax import lax
from jax.sharding import PartitionSpec as P

root_coef = 0.7978845608028654
cubic_coef = 0.044715
n_chunk = 2


def gelu_slope(pre_act):
    inner_arg = root_coef * (pre_act + cubic_coef * pre_act * pre_act * pre_act)
    tangent = jnp.tanh(inner_arg)
    return 0.5 * (1.0 + tangent) + 0.5 * pre_act * (1.0 - tangent * tangent) * root_coef * (
        1.0 + 3.0 * cubic_coef * pre_act * pre_act
    )


def place_slots(route_block, experts, capacity):
    tok_count = route_block.shape[0]
    ordered = jnp.transpose(route_block).reshape(-1)
    onehot = (ordered[:, None] == jnp.arange(experts, dtype=jnp.int32)[None, :]).astype(jnp.int32)
    before = jnp.cumsum(onehot, axis=0) - onehot
    position = jnp.sum(before * onehot, axis=1)
    return (
        jnp.transpose(ordered.reshape(2, tok_count)),
        jnp.transpose(position.reshape(2, tok_count)),
    )


def swap_pairs(back):
    pairs = []
    for b in range(4):
        for d in range(4):
            for core in range(2):
                at_batch = (d * 2 + core) * 4 + b
                at_part = (((d - b) % 4) * 2 + core) * 4 + d
                pairs.append((at_part, at_batch) if back else (at_batch, at_part))
    return pairs


def shift(block, step):
    return lax.ppermute(block, "dp", [(i, i + step) for i in range(4) if 0 <= i + step < 4])


def per_device(tokens, routes, up_weight, saved_pre, grad_act):
    experts = lax.axis_size("expert")
    place = lax.axis_index("dp")
    slot_count, hidden = saved_pre.shape[1:]
    capacity = slot_count // experts
    part = capacity // n_chunk
    tok_dev, width = tokens.shape
    weight = up_weight[0]

    def unit_of(c):
        pre = saved_pre[0].reshape(experts, capacity, hidden)[:, c * part : (c + 1) * part]
        act = grad_act[0].reshape(experts, capacity, hidden)[:, c * part : (c + 1) * part]
        unit = act.astype(jnp.float32) * gelu_slope(pre.astype(jnp.float32))
        return unit.astype(jnp.bfloat16).reshape(experts * part, hidden)

    units = []
    for c in range(n_chunk):
        own = unit_of(c)
        right, left = [own], [own]
        for step in range(3):
            right.append(shift(right[-1], 1))
            left.append(shift(left[-1], -1))
        units.append(
            [own] + [jnp.where(place >= j, right[j], left[4 - j]) for j in range(1, 4)]
        )

    expert_of, position = place_slots(routes, experts, capacity)
    slot_index = expert_of * capacity + position
    token_ids = jnp.broadcast_to(
        jnp.arange(tok_dev, dtype=jnp.int32)[:, None], (tok_dev, 2)
    ).reshape(-1)
    holder = jnp.zeros((slot_count,), jnp.int32).at[slot_index.reshape(-1)].set(token_ids + 1)
    filled = holder > 0
    source_row = jnp.maximum(holder - 1, 0)
    nothing = jnp.zeros((), jnp.bfloat16)
    outgoing = jnp.where(filled[:, None], jnp.take(tokens, source_row, axis=0), nothing)
    arrived = lax.all_to_all(outgoing, "expert", split_axis=0, concat_axis=0, tiled=True)
    arrived = lax.ppermute(arrived, ("tensor", "dp"), swap_pairs(False))
    rows = lax.all_gather(arrived, "tensor", axis=0, tiled=False)
    rows = rows.reshape(4, 2, experts, n_chunk, part, width)

    returned = []
    grad_total = jnp.zeros((), jnp.float32)
    for c in range(n_chunk):
        block = jnp.concatenate(units[c], axis=0)
        partial = lax.dot_general(
            block, weight, (((1,), (1,)), ((), ())), preferred_element_type=jnp.float32
        ).astype(jnp.bfloat16)
        partial = jnp.transpose(partial.reshape(4, experts * part, 2, width), (0, 2, 1, 3))
        summed = lax.psum_scatter(
            partial.reshape(8, experts * part, width), "tensor", scatter_dimension=0, tiled=False
        )
        summed = lax.ppermute(summed, ("tensor", "dp"), swap_pairs(True))
        returned.append(
            lax.all_to_all(summed, "expert", split_axis=0, concat_axis=0, tiled=True)
        )
        rows_c = jnp.transpose(rows[:, :, :, c], (0, 2, 3, 1, 4)).reshape(-1, 2 * width)
        grad_total = grad_total + lax.dot_general(
            rows_c, block, (((0,), (0,)), ((), ())), preferred_element_type=jnp.float32
        )
    grad_block = grad_total.astype(jnp.bfloat16)
    returned = jnp.concatenate(returned, axis=0)
    where_slot = (
        (position // part) * (experts * part) + expert_of * part + position % part
    )
    first_part = jnp.take(returned, where_slot[:, 0], axis=0).astype(jnp.float32)
    second = jnp.take(returned, where_slot[:, 1], axis=0).astype(jnp.float32)
    token_grad = (first_part + second).astype(jnp.bfloat16)
    return (token_grad, grad_block[None])


def solution(mesh):
    placed = (
        P(("expert", "dp"), "tensor"),
        P(("expert", "dp"), None),
        P("expert", "dp", "tensor"),
        P("expert", "dp", "tensor"),
        P("expert", "dp", "tensor"),
    )
    return jax.shard_map(
        per_device,
        mesh=mesh,
        in_specs=placed,
        out_specs=(P(("expert", "dp"), "tensor"), P("expert", "dp", "tensor")),
        check_vma=False,
    )
```

time: 591 us -> 338 us (0.57)
  waiting for transfers between devices: 488 us -> 137 us
  starting transfers between devices: 19.5 us -> 64.5 us
  local copies, waits for them, and re-layouts: 14.4 us -> 36.3 us
  blocking collectives: 14.3 us -> 33 us
  other arithmetic: 7.82 us -> 17 us
    all_gather x1, waiting for transfers between devices: 253 us -> 16.5 us  [per_device(): rows = lax.all_gather(arrived, 'tensor', axis=0, tiled=False)]
    reduce_scatter x1 -> x2, waiting for transfers between devices: 194 us -> 0.04 us  [per_device(): lax.psum_scatter(partial.reshape(8, experts * part, width), 'tensor', sca...]
    ppermute x0 -> x15, waiting for transfers between devices: none -> 121 us  [the longest x12 107 us: shift(): lax.ppermute(block, 'dp', [(i, i + step) for i in range(4) if 0 <= i + st...]
    ppermute x0 -> x15, starting transfers between devices: none -> 42.9 us  [the longest x12 37.2 us: shift(): lax.ppermute(block, 'dp', [(i, i + step) for i in range(4) if 0 <= i + st...]
    all_to_all x0 -> x1, blocking collectives: none -> 33 us  [per_device(): lax.all_to_all(outgoing, 'expert', split_axis=0, concat_axis=0, tiled=True)]
    unnamed x4 -> x3, waiting for transfers between devices: 26.5 us -> 0.05 us
    reshape x0 -> x4, local copies, waits for them, and re-layouts: none -> 14.4 us  [per_device(): partial.reshape(4, experts * part, 2, width)]
    all_gather x1 -> x0, blocking collectives: 14.3 us -> none  [per_device(): gathered = lax.all_gather(tokens, 'tensor', axis=1, tiled=True)]
  transfers between devices with their start and end apart: 5 -> 20, of which waited for: 4 -> 10; matrix products, arithmetic and copies ran while one was open for 9% -> 20% of each run, Pallas kernels for 0% -> 0%
where the time goes in v1:
time: 338 us; the launch traced here: 333 us
  waiting for transfers between devices  137 us (41%)
  starting transfers between devices  64.5 us (19%)
  local copies, waits for them, and re-layouts  36.3 us (11%)
  blocking collectives  33 us (10%)
  matrix products  30.4 us (9%)
  other arithmetic  17 us (5%)
  between operations  14.2 us (4%)
    ppermute x12, waiting for transfers between devices, shift(): lax.ppermute(block, 'dp', [(i, i + step) for i in range(4) if 0 <= i + st...  107 us
    ppermute x12, starting transfers between devices, shift(): lax.ppermute(block, 'dp', [(i, i + step) for i in range(4) if 0 <= i + st...  37.2 us
    all_to_all x1, blocking collectives, per_device(): lax.all_to_all(outgoing, 'expert', split_axis=0, concat_axis=0, tiled=True)  33 us
    all_to_all x2, starting transfers between devices, per_device(): lax.all_to_all(summed, 'expert', split_axis=0, concat_axis=0, tiled=True)  21.5 us
    dot_general x2, matrix products, per_device(): lax.dot_general(rows_c, block, (((0,), (0,)), ((), ())), preferred_elemen...  17.1 us
    all_gather x1, waiting for transfers between devices, per_device(): rows = lax.all_gather(arrived, 'tensor', axis=0, tiled=False)  16.5 us
    reshape x4, local copies, waits for them, and re-layouts, per_device(): partial.reshape(4, experts * part, 2, width)  14.4 us
    dot_general x2, matrix products, per_device(): lax.dot_general(block, weight, (((1,), (1,)), ((), ())), preferred_elemen...  13.3 us
  transfers between devices with their start and end apart: 20, of which 10 were waited for; matrix products, arithmetic and copies ran while one was open for 20% of the time, Pallas kernels for 0%

profile of v1, /device:TPU:166, one launch (start us, length us, event | category | flops | bytes accessed | tf_op | source)
XLA Modules:
  0.0 332.7 jit_solution(14056089166691579098)
XLA Ops:
  7.2 5.4 %fusion.12 = (bf16[8,32,2048]{2,1,0:T(8,128)(2,1)S(1)}, bf16[8,32,2048]{2,1,0:T(8,128)(2,1)}) fusion(bf16[8,64,2048]{2,1,0:T(8,128)(2,1)} %bitcast.87, bf16[8,64,2048]{2,1,0:T(8,128)(2,1)} %bitcast.88), kind=kLoop, calls=%fused_computation.33 | loop fusion | flops 22020096 | bytes 6291456 | tf_op jit(solution)/shard_map/convert_element_type | solution.py:59
  12.6 2.9 collective-permute-start.1
  15.6 2.9 collective-permute-start
  18.5 20.9 %collective-permute-done.1 = bf16[256,2048]{1,0:T(8,128)(2,1)S(1)} collective-permute-done((bf16[256,2048]{1,0:T(8,128)(2,1)S(1)}, bf16[256,2048]{1,0:T(8,128)(2,1)S(1)}, u32[]{:S(2)}, u32[]{:S(2)}) %collective-permute-start.1) | collective-permute-done | bytes 1048608 | tf_op jit(solution)/shard_map/ppermute | solution.py:43
  39.4 1.0 copy-done.11
  40.4 2.9 collective-permute-start.2
  43.3 1.9 collective-permute-start.8
  45.2 3.9 %collective-permute-start.7 = (bf16[256,2048]{1,0:T(8,128)(2,1)}, bf16[256,2048]{1,0:T(8,128)(2,1)}, u32[]{:S(2)}, u32[]{:S(2)}) collective-permute-start(bf16[256,2048]{1,0:T(8,128)(2,1)} %bitcast.17), channel_id=1, source_target_pairs={{0,1},{1,2},{2,3},{4,5},{5,6},{6,7},{8,9},{9,10},{10,11},{12,13},{... | collective-permute-start | bytes 3145736 | tf_op jit(solution)/shard_map/ppermute | solution.py:43
  49.2 3.9 %collective-permute-start.4 = (bf16[256,2048]{1,0:T(8,128)(2,1)}, bf16[256,2048]{1,0:T(8,128)(2,1)}, u32[]{:S(2)}, u32[]{:S(2)}) collective-permute-start(bf16[256,2048]{1,0:T(8,128)(2,1)} %collective-permute-done), channel_id=1, source_target_pairs={{0,1},{1,2},{2,3},{4,5},{5,6},{6,7},{8,9},{9,10},{10,11},{12,13},{... | collective-permute-start | bytes 3145736 | tf_op jit(solution)/shard_map/ppermute | solution.py:43
  53.1 15.4 %collective-permute-done.2 = bf16[256,2048]{1,0:T(8,128)(2,1)} collective-permute-done((bf16[256,2048]{1,0:T(8,128)(2,1)S(1)}, bf16[256,2048]{1,0:T(8,128)(2,1)}, u32[]{:S(2)}, u32[]{:S(2)}) %collective-permute-start.2) | collective-permute-done | bytes 1048608 | tf_op jit(solution)/shard_map/ppermute | solution.py:43
  68.5 2.9 collective-permute-start.3
  71.4 19.5 %collective-permute-done.8 = bf16[256,2048]{1,0:T(8,128)(2,1)} collective-permute-done((bf16[256,2048]{1,0:T(8,128)(2,1)}, bf16[256,2048]{1,0:T(8,128)(2,1)}, u32[]{:S(2)}, u32[]{:S(2)}) %collective-permute-start.8) | collective-permute-done | bytes 1048608 | tf_op jit(solution)/shard_map/ppermute | solution.py:43
  90.9 2.9 collective-permute-start.9
  93.9 2.9 collective-permute-start.11
  96.8 3.9 %collective-permute-start.5 = (bf16[256,2048]{1,0:T(8,128)(2,1)}, bf16[256,2048]{1,0:T(8,128)(2,1)S(1)}, u32[]{:S(2)}, u32[]{:S(2)}) collective-permute-start(bf16[256,2048]{1,0:T(8,128)(2,1)} %collective-permute-done.4), channel_id=1, source_target_pairs={{0,1},{1,2},{2,3},{4,5},{5,6},{6,7},{8,9},{9,10},{10,11},{12,13},{... | collective-permute-start | bytes 3145736 | tf_op jit(solution)/shard_map/ppermute | solution.py:43
  100.7 1.4 broadcast_select_fusion.3
  102.1 11.3 %collective-permute-done.3 = bf16[256,2048]{1,0:T(8,128)(2,1)} collective-permute-done((bf16[256,2048]{1,0:T(8,128)(2,1)}, bf16[256,2048]{1,0:T(8,128)(2,1)}, u32[]{:S(2)}, u32[]{:S(2)}) %collective-permute-start.3) | collective-permute-done | bytes 1048608 | tf_op jit(solution)/shard_map/ppermute | solution.py:43
  113.4 1.3 broadcast_select_fusion.5
  114.8 24.4 %collective-permute-done.5 = bf16[256,2048]{1,0:T(8,128)(2,1)S(1)} collective-permute-done((bf16[256,2048]{1,0:T(8,128)(2,1)}, bf16[256,2048]{1,0:T(8,128)(2,1)S(1)}, u32[]{:S(2)}, u32[]{:S(2)}) %collective-permute-start.5) | collective-permute-done | bytes 1048608 | tf_op jit(solution)/shard_map/ppermute | solution.py:43
  139.3 1.0 copy-done.4
  140.4 7.5 %fusion.23 = bf16[1024,768]{1,0:T(8,128)(2,1)} fusion(bf16[1,768,2048]{2,1,0:T(8,128)(2,1)S(1)} %copy-done, bf16[256,2048]{1,0:T(8,128)(2,1)S(1)} %broadcast_select_fusion.1, bf16[256,2048]{1,0:T(8,128)(2,1)S(1)} %broadcast_select_fusion.3, bf16[256,2048]{1,0:T(8,128)(2,1)S(1)} %broadcast_select_fusion.5, bf16[256,2048]{1,0:T(8,128)(2,1)S(1)} %bitcast.95), kind=kOutput, calls=%fused_computation.44 | convolution fusion | flops 3238789120 | bytes 8912896 | tf_op jit(solution)/shard_map/dot_general | solution.py:91
  147.8 4.4 %reshape.114 = bf16[4,256,2,384]{3,2,1,0:T(2,128)(2,1)} reshape(bf16[1024,768]{1,0:T(8,128)(2,1)} %fusion.23) | data formatting | bytes 3145728 | tf_op jit(solution)/shard_map/reshape | solution.py:94
  152.2 2.8 copy.11
  155.1 1.9 collective-permute-start.10
  157.0 4.1 %collective-permute-start.12 = (bf16[256,2048]{1,0:T(8,128)(2,1)}, bf16[256,2048]{1,0:T(8,128)(2,1)S(1)}, u32[]{:S(2)}, u32[]{:S(2)}) collective-permute-start(bf16[256,2048]{1,0:T(8,128)(2,1)} %collective-permute-done.11), channel_id=1, source_target_pairs={{0,1},{1,2},{2,3},{4,5},{5,6},{6,7},{8,9},{9,10},{10,11},{12,13},{... | collective-permute-start | bytes 3145736 | tf_op jit(solution)/shard_map/ppermute | solution.py:43
  161.2 1.4 broadcast_select_fusion.2
  162.5 14.6 %collective-permute-done.10 = bf16[256,2048]{1,0:T(8,128)(2,1)S(1)} collective-permute-done((bf16[256,2048]{1,0:T(8,128)(2,1)}, bf16[256,2048]{1,0:T(8,128)(2,1)S(1)}, u32[]{:S(2)}, u32[]{:S(2)}) %collective-permute-start.10) | collective-permute-done | bytes 1048608 | tf_op jit(solution)/shard_map/ppermute | solution.py:43
  177.1 1.3 broadcast_select_fusion.4
  178.5 0.6 collective-permute-done.12
  179.0 1.4 broadcast_select_fusion
  180.5 1.0 copy-done.9
  181.4 5.8 %fusion.26 = bf16[1024,768]{1,0:T(8,128)(2,1)} fusion(bf16[1,768,2048]{2,1,0:T(8,128)(2,1)S(1)} %copy-done, bf16[256,2048]{1,0:T(8,128)(2,1)S(1)} %broadcast_select_fusion, bf16[256,2048]{1,0:T(8,128)(2,1)S(1)} %broadcast_select_fusion.2, bf16[256,2048]{1,0:T(8,128)(2,1)S(1)} %broadcast_select_fusion.4, bf16[256,2048]{1,0:T(8,128)(2,1)} %bitcast.17), kind=kOutput, calls=%fused_computation.45 | convolution fusion | flops 3238789120 | bytes 8912896 | tf_op jit(solution)/shard_map/dot_general | solution.py:91
  187.3 4.4 %reshape.117 = bf16[4,256,2,384]{3,2,1,0:T(2,128)(2,1)} reshape(bf16[1024,768]{1,0:T(8,128)(2,1)} %fusion.26) | data formatting | bytes 3145728 | tf_op jit(solution)/shard_map/reshape | solution.py:94
  191.6 2.8 copy.12
  194.5 0.6 reduce-window.6
  196.0 1.4 scatter_custom_fusion
  197.6 2.6 gather_fusion
  200.2 1.2 select_select_fusion
  201.4 33.0 %all_to_all.33 = bf16[8,64,384]{2,1,0:T(8,128)(2,1)S(1)} all-to-all(bf16[8,64,384]{2,1,0:T(8,128)(2,1)S(1)} %select_select_fusion), channel_id=1, replica_groups=mesh['tensor'=8,'expert'=8,'dp'=4] {'expert'}, dimensions={0} | all-to-all | bytes 786432 | tf_op jit(solution)/shard_map/all_to_all | solution.py:82
  234.4 1.9 collective-permute-start.14
  236.3 7.7 %collective-permute-done.14 = bf16[512,384]{1,0:T(8,128)(2,1)S(1)} collective-permute-done((bf16[512,384]{1,0:T(8,128)(2,1)S(1)}, bf16[512,384]{1,0:T(8,128)(2,1)S(1)}, u32[]{:S(2)}, u32[]{:S(2)}) %collective-permute-start.14) | collective-permute-done | bytes 393248 | tf_op jit(solution)/shard_map/ppermute | solution.py:83
  244.1 0.8 copy-done.17
  244.9 1.9 collective-permute-start.6
  246.9 1.9 collective-permute-start.13
  248.8 6.3 %collective-permute-done.6 = bf16[256,384]{1,0:T(8,128)(2,1)} collective-permute-done((bf16[256,384]{1,0:T(8,128)(2,1)}, bf16[256,384]{1,0:T(8,128)(2,1)}, u32[]{:S(2)}, u32[]{:S(2)}) %collective-permute-start.6) | collective-permute-done | bytes 196640 | tf_op jit(solution)/shard_map/ppermute | solution.py:98
  255.1 11.9 %all-to-all-start = ((bf16[8,32,384]{2,1,0:T(8,128)(2,1)}), bf16[8,32,384]{2,1,0:T(8,128)(2,1)S(1)}, u32[]{:S(2)}, u32[]{:S(2)}) async-start(bf16[8,32,384]{2,1,0:T(8,128)(2,1)} %bitcast.15), calls=%async_computation.1 | async-start | bytes 393216 | tf_op jit(solution)/shard_map/all_to_all | solution.py:100
  266.9 16.5 %all-gather.3.cloned.1.call-done = bf16[4096,384]{1,0:T(8,128)(2,1)} async-done(((bf16[512,384]{1,0:T(8,128)(2,1)}), bf16[4096,384]{1,0:T(8,128)(2,1)}) %all-gather.3.cloned.1.call-update) | async-done | bytes 3145744 | tf_op jit(solution)/shard_map/all_gather | solution.py:84
  283.4 2.3 slice_bitcast_fusion.1
  285.7 1.6 copy.16
  287.3 0.3 copy.18
  287.7 0.9 copy-done.6
  288.5 0.3 copy-done.8
  288.9 0.3 copy-done.10
  289.2 7.5 %fusion.29 = f32[768,2048]{1,0:T(8,128)} fusion(bf16[1024,768]{1,0:T(8,128)(2,1)S(1)} %bitcast.90, bf16[256,2048]{1,0:T(8,128)(2,1)S(1)} %copy-done.10, bf16[256,2048]{1,0:T(8,128)(2,1)S(1)} %copy-done.6, bf16[256,2048]{1,0:T(8,128)(2,1)S(1)} %copy-done.8, bf16[256,2048]{1,0:T(8,128)(2,1)} %bitcast.17), kind=kOutput, calls=%fused_computation.54 | convolution fusion | flops 3238002688 | bytes 12058624 | tf_op jit(solution)/shard_map/dot_general | solution.py:103
  296.6 1.6 copy.15
  298.3 1.5 copy.17
  299.8 0.7 copy-done.18
  300.5 9.6 %all-to-all-start.1 = ((bf16[8,32,384]{2,1,0:T(8,128)(2,1)}), bf16[8,32,384]{2,1,0:T(8,128)(2,1)S(1)}, u32[]{:S(2)}, u32[]{:S(2)}) async-start(bf16[8,32,384]{2,1,0:T(8,128)(2,1)} %bitcast.99), calls=%async_computation.3 | async-start | bytes 393216 | tf_op jit(solution)/shard_map/all_to_all | solution.py:100
  310.1 9.7 %fusion.4 = bf16[1,768,2048]{2,1,0:T(8,128)(2,1)} fusion(f32[768,2048]{1,0:T(8,128)} %fusion.29, bf16[1024,768]{1,0:T(8,128)(2,1)} %bitcast.89, bf16[256,2048]{1,0:T(8,128)(2,1)} %copy-done.4, bf16[256,2048]{1,0:T(8,128)(2,1)} %copy-done.2, bf16[256,2048]{1,0:T(8,128)(2,1)} %copy-done.3, bf16[256,2048]{1,0:T(8,128)(2,1)} %bitcast.94), kind=kOutput, calls=%fused_computation.25 | convolution fusion | flops 3241148416 | bytes 15204352 | tf_op jit(solution)/shard_map/dot_general | solution.py:103
  319.8 0.7 copy-done.16
  320.5 1.1 pad_maximum_fusion.6
  321.5 1.5 gather_fusion.2
  323.0 1.5 gather_fusion.1
  324.5 1.7 add_convert_fusion.1
  (67 shorter events, 1.5 us)
Async XLA Ops:
  7.2 133.2 %copy-start = (bf16[1,768,2048]{2,1,0:T(8,128)(2,1)S(1)}, bf16[1,768,2048]{2,1,0:T(8,128)(2,1)}, u32[]{:S(2)}) copy-start(bf16[1,768,2048]{2,1,0:T(8,128)(2,1)} %param.9) | copy-start | bytes 9437188
  7.2 237.7 %reduce-scatter.3.cloned.1.call-start = ((), (), s32[]{:S(2)}) async-start(), calls=%async_computation.5 | async-start | bytes 1769472 | tf_op jit(solution)/shard_map/reduce_scatter | solution.py:95
  12.6 55.8 %copy-start.13 = (bf16[8,32,2048]{2,1,0:T(8,128)(2,1)}, bf16[8,32,2048]{2,1,0:T(8,128)(2,1)S(1)}, u32[]{:S(2)}) copy-start(bf16[8,32,2048]{2,1,0:T(8,128)(2,1)S(1)} %get-tuple-element.7) | copy-start | bytes 3145732
  12.6 26.8 %collective-permute-start.1 = (bf16[256,2048]{1,0:T(8,128)(2,1)S(1)}, bf16[256,2048]{1,0:T(8,128)(2,1)S(1)}, u32[]{:S(2)}, u32[]{:S(2)}) collective-permute-start(bf16[256,2048]{1,0:T(8,128)(2,1)S(1)} %bitcast.92), channel_id=1, source_target_pairs={{1,0},{2,1},{3,2},{5,4},{6,5},{7,6},{9,8},{10,9},{11,10},{13,12},{... | collective-permute-start | bytes 3145736 | tf_op jit(solution)/shard_map/ppermute | solution.py:43
  15.6 33.6 %collective-permute-start = (bf16[256,2048]{1,0:T(8,128)(2,1)S(1)}, bf16[256,2048]{1,0:T(8,128)(2,1)}, u32[]{:S(2)}, u32[]{:S(2)}) collective-permute-start(bf16[256,2048]{1,0:T(8,128)(2,1)S(1)} %bitcast.93), channel_id=1, source_target_pairs={{0,1},{1,2},{2,3},{4,5},{5,6},{6,7},{8,9},{9,10},{10,11},{12,13},{... | collective-permute-start | bytes 3145736 | tf_op jit(solution)/shard_map/ppermute | solution.py:43
  39.4 1.0 copy-start.11
  40.4 28.1 %collective-permute-start.2 = (bf16[256,2048]{1,0:T(8,128)(2,1)S(1)}, bf16[256,2048]{1,0:T(8,128)(2,1)}, u32[]{:S(2)}, u32[]{:S(2)}) collective-permute-start(bf16[256,2048]{1,0:T(8,128)(2,1)S(1)} %collective-permute-done.1), channel_id=1, source_target_pairs={{1,0},{2,1},{3,2},{5,4},{6,5},{7,6},{9,8},{10,9},{11,10},{13,12},{... | collective-permute-start | bytes 3145736 | tf_op jit(solution)/shard_map/ppermute | solution.py:43
  43.3 47.6 %collective-permute-start.8 = (bf16[256,2048]{1,0:T(8,128)(2,1)}, bf16[256,2048]{1,0:T(8,128)(2,1)}, u32[]{:S(2)}, u32[]{:S(2)}) collective-permute-start(bf16[256,2048]{1,0:T(8,128)(2,1)} %bitcast.17), channel_id=1, source_target_pairs={{1,0},{2,1},{3,2},{5,4},{6,5},{7,6},{9,8},{10,9},{11,10},{13,12},{... | collective-permute-start | bytes 3145736 | tf_op jit(solution)/shard_map/ppermute | solution.py:43
  45.2 48.6 %collective-permute-start.7 = (bf16[256,2048]{1,0:T(8,128)(2,1)}, bf16[256,2048]{1,0:T(8,128)(2,1)}, u32[]{:S(2)}, u32[]{:S(2)}) collective-permute-start(bf16[256,2048]{1,0:T(8,128)(2,1)} %bitcast.17), channel_id=1, source_target_pairs={{0,1},{1,2},{2,3},{4,5},{5,6},{6,7},{8,9},{9,10},{10,11},{12,13},{... | collective-permute-start | bytes 3145736 | tf_op jit(solution)/shard_map/ppermute | solution.py:43
  49.2 47.6 %collective-permute-start.4 = (bf16[256,2048]{1,0:T(8,128)(2,1)}, bf16[256,2048]{1,0:T(8,128)(2,1)}, u32[]{:S(2)}, u32[]{:S(2)}) collective-permute-start(bf16[256,2048]{1,0:T(8,128)(2,1)} %collective-permute-done), channel_id=1, source_target_pairs={{0,1},{1,2},{2,3},{4,5},{5,6},{6,7},{8,9},{9,10},{10,11},{12,13},{... | collective-permute-start | bytes 3145736 | tf_op jit(solution)/shard_map/ppermute | solution.py:43
  68.5 44.9 %collective-permute-start.3 = (bf16[256,2048]{1,0:T(8,128)(2,1)}, bf16[256,2048]{1,0:T(8,128)(2,1)}, u32[]{:S(2)}, u32[]{:S(2)}) collective-permute-start(bf16[256,2048]{1,0:T(8,128)(2,1)} %collective-permute-done.2), channel_id=1, source_target_pairs={{1,0},{2,1},{3,2},{5,4},{6,5},{7,6},{9,8},{10,9},{11,10},{13,12},{... | collective-permute-start | bytes 3145736 | tf_op jit(solution)/shard_map/ppermute | solution.py:43
  90.9 64.1 %collective-permute-start.9 = (bf16[256,2048]{1,0:T(8,128)(2,1)}, bf16[256,2048]{1,0:T(8,128)(2,1)}, u32[]{:S(2)}, u32[]{:S(2)}) collective-permute-start(bf16[256,2048]{1,0:T(8,128)(2,1)} %collective-permute-done.8), channel_id=1, source_target_pairs={{1,0},{2,1},{3,2},{5,4},{6,5},{7,6},{9,8},{10,9},{11,10},{13,12},{... | collective-permute-start | bytes 3145736 | tf_op jit(solution)/shard_map/ppermute | solution.py:43
  93.9 63.2 %collective-permute-start.11 = (bf16[256,2048]{1,0:T(8,128)(2,1)}, bf16[256,2048]{1,0:T(8,128)(2,1)}, u32[]{:S(2)}, u32[]{:S(2)}) collective-permute-start(bf16[256,2048]{1,0:T(8,128)(2,1)} %collective-permute-done.7), channel_id=1, source_target_pairs={{0,1},{1,2},{2,3},{4,5},{5,6},{6,7},{8,9},{9,10},{10,11},{12,13},{... | collective-permute-start | bytes 3145736 | tf_op jit(solution)/shard_map/ppermute | solution.py:43
  96.8 42.4 %collective-permute-start.5 = (bf16[256,2048]{1,0:T(8,128)(2,1)}, bf16[256,2048]{1,0:T(8,128)(2,1)S(1)}, u32[]{:S(2)}, u32[]{:S(2)}) collective-permute-start(bf16[256,2048]{1,0:T(8,128)(2,1)} %collective-permute-done.4), channel_id=1, source_target_pairs={{0,1},{1,2},{2,3},{4,5},{5,6},{6,7},{8,9},{9,10},{10,11},{12,13},{... | collective-permute-start | bytes 3145736 | tf_op jit(solution)/shard_map/ppermute | solution.py:43
  102.1 37.2 %copy-start.2 = (bf16[256,2048]{1,0:T(8,128)(2,1)}, bf16[256,2048]{1,0:T(8,128)(2,1)S(1)}, u32[]{:S(2)}) copy-start(bf16[256,2048]{1,0:T(8,128)(2,1)S(1)} %broadcast_select_fusion.3) | copy-start | bytes 3145732
  102.1 37.1 %copy-start.12 = (bf16[256,2048]{1,0:T(8,128)(2,1)S(1)}, bf16[256,2048]{1,0:T(8,128)(2,1)}, u32[]{:S(2)}) copy-start(bf16[256,2048]{1,0:T(8,128)(2,1)} %copy-done.11) | copy-start | bytes 3145732
  114.8 24.6 %copy-start.3 = (bf16[256,2048]{1,0:T(8,128)(2,1)}, bf16[256,2048]{1,0:T(8,128)(2,1)S(1)}, u32[]{:S(2)}) copy-start(bf16[256,2048]{1,0:T(8,128)(2,1)S(1)} %broadcast_select_fusion.5) | copy-start | bytes 3145732
  114.8 25.6 %copy-start.14 = (bf16[8,32,2048]{2,1,0:T(8,128)(2,1)S(1)}, bf16[8,32,2048]{2,1,0:T(8,128)(2,1)}, u32[]{:S(2)}) copy-start(bf16[8,32,2048]{2,1,0:T(8,128)(2,1)} %copy-done.13) | copy-start | bytes 3145732
  139.3 1.0 copy-start.4
  155.0 91.8 %reduce-scatter.5.cloned.1.call-start = ((), (), s32[]{:S(2)}) async-start(), calls=%async_computation.6 | async-start | bytes 1769472 | tf_op jit(solution)/shard_map/reduce_scatter | solution.py:95
  155.1 22.0 %collective-permute-start.10 = (bf16[256,2048]{1,0:T(8,128)(2,1)}, bf16[256,2048]{1,0:T(8,128)(2,1)S(1)}, u32[]{:S(2)}, u32[]{:S(2)}) collective-permute-start(bf16[256,2048]{1,0:T(8,128)(2,1)} %collective-permute-done.9), channel_id=1, source_target_pairs={{1,0},{2,1},{3,2},{5,4},{6,5},{7,6},{9,8},{10,9},{11,10},{13,12},{... | collective-permute-start | bytes 3145736 | tf_op jit(solution)/shard_map/ppermute | solution.py:43
  157.0 22.0 %collective-permute-start.12 = (bf16[256,2048]{1,0:T(8,128)(2,1)}, bf16[256,2048]{1,0:T(8,128)(2,1)S(1)}, u32[]{:S(2)}, u32[]{:S(2)}) collective-permute-start(bf16[256,2048]{1,0:T(8,128)(2,1)} %collective-permute-done.11), channel_id=1, source_target_pairs={{0,1},{1,2},{2,3},{4,5},{5,6},{6,7},{8,9},{9,10},{10,11},{12,13},{... | collective-permute-start | bytes 3145736 | tf_op jit(solution)/shard_map/ppermute | solution.py:43
  162.5 17.9 %copy-start.5 = (bf16[256,2048]{1,0:T(8,128)(2,1)}, bf16[256,2048]{1,0:T(8,128)(2,1)S(1)}, u32[]{:S(2)}) copy-start(bf16[256,2048]{1,0:T(8,128)(2,1)S(1)} %broadcast_select_fusion.2) | copy-start | bytes 3145732
  178.5 2.0 copy-start.7
  180.4 1.0 copy-start.9
  191.6 2.9 copy-start.19
  191.6 6.0 %copy-start.1 = (bf16[128,384]{1,0:T(8,128)(2,1)S(1)}, bf16[128,384]{1,0:T(8,128)(2,1)}, u32[]{:S(2)}) copy-start(bf16[128,384]{1,0:T(8,128)(2,1)} %param.7) | copy-start | bytes 294916
  194.5 88.9 %all-gather.3.cloned.1.call-start = ((), (), s32[]{:S(2)}) async-start(), calls=%async_computation.7 | async-start | bytes 3538944 | tf_op jit(solution)/shard_map/all_gather | solution.py:84
  234.4 9.7 %collective-permute-start.14 = (bf16[512,384]{1,0:T(8,128)(2,1)S(1)}, bf16[512,384]{1,0:T(8,128)(2,1)S(1)}, u32[]{:S(2)}, u32[]{:S(2)}) collective-permute-start(bf16[512,384]{1,0:T(8,128)(2,1)S(1)} %bitcast.98), channel_id=1, source_target_pairs={{0,0},{32,32},{64,65},{96,97},{128,130},{160,162},{192,195},{224,2... | collective-permute-start | bytes 1179656 | tf_op jit(solution)/shard_map/ppermute | solution.py:83
  244.1 0.8 copy-start.17
  244.9 10.2 %collective-permute-start.6 = (bf16[256,384]{1,0:T(8,128)(2,1)}, bf16[256,384]{1,0:T(8,128)(2,1)}, u32[]{:S(2)}, u32[]{:S(2)}) collective-permute-start(bf16[256,384]{1,0:T(8,128)(2,1)} %bitcast.103), channel_id=1, source_target_pairs={{0,0},{32,32},{65,64},{97,96},{130,128},{162,160},{195,192},{227,2... | collective-permute-start | bytes 589832 | tf_op jit(solution)/shard_map/ppermute | solution.py:98
  246.9 52.9 %collective-permute-start.13 = (bf16[256,384]{1,0:T(8,128)(2,1)}, bf16[256,384]{1,0:T(8,128)(2,1)S(1)}, u32[]{:S(2)}, u32[]{:S(2)}) collective-permute-start(bf16[256,384]{1,0:T(8,128)(2,1)} %bitcast.104), channel_id=1, source_target_pairs={{0,0},{32,32},{65,64},{97,96},{130,128},{162,160},{195,192},{227,2... | collective-permute-start | bytes 589832 | tf_op jit(solution)/shard_map/ppermute | solution.py:98
  255.1 44.7 %all-to-all-start = ((bf16[8,32,384]{2,1,0:T(8,128)(2,1)}), bf16[8,32,384]{2,1,0:T(8,128)(2,1)S(1)}, u32[]{:S(2)}, u32[]{:S(2)}) async-start(bf16[8,32,384]{2,1,0:T(8,128)(2,1)} %bitcast.15), calls=%async_computation.1 | async-start | bytes 393216 | tf_op jit(solution)/shard_map/all_to_all | solution.py:100
  287.3 1.2 copy-start.6
  287.3 1.5 copy-start.8
  287.3 1.8 copy-start.10
  299.8 0.7 copy-start.18
  300.5 19.3 %copy-start.15 = (bf16[8,32,384]{2,1,0:T(8,128)(2,1)}, bf16[8,32,384]{2,1,0:T(8,128)(2,1)S(1)}, u32[]{:S(2)}) copy-start(bf16[8,32,384]{2,1,0:T(8,128)(2,1)S(1)} %all-to-all-done) | copy-start | bytes 589828
  300.5 19.3 %all-to-all-start.1 = ((bf16[8,32,384]{2,1,0:T(8,128)(2,1)}), bf16[8,32,384]{2,1,0:T(8,128)(2,1)S(1)}, u32[]{:S(2)}, u32[]{:S(2)}) async-start(bf16[8,32,384]{2,1,0:T(8,128)(2,1)} %bitcast.99), calls=%async_computation.3 | async-start | bytes 393216 | tf_op jit(solution)/shard_map/all_to_all | solution.py:100
  319.8 0.7 copy-start.16
Sparse Core Ops, SparseCore 0:
  155.2 36.2 reduce-scatter.2
  194.6 38.0 reduce-scatter.4
  245.0 38.3 all-gather.2

commit v2 on v0

v2 whole, which is shorter than its diff:
```python
import functools

import jax
import jax.numpy as jnp
from jax import lax
from jax.experimental import pallas as pl
from jax.experimental.pallas import tpu as pltpu
from jax.sharding import PartitionSpec as P

root_coef = 0.7978845608028654
cubic_coef = 0.044715
n_chunk = 2
n_x, n_y, n_dp = 4, 4, 4
f32, bf16 = jnp.float32, jnp.bfloat16


def gelu_slope(pre_act):
    inner_arg = root_coef * (pre_act + cubic_coef * pre_act * pre_act * pre_act)
    tangent = jnp.tanh(inner_arg)
    return 0.5 * (1.0 + tangent) + 0.5 * pre_act * (1.0 - tangent * tangent) * root_coef * (
        1.0 + 3.0 * cubic_coef * pre_act * pre_act
    )


def place_slots(route_block, experts):
    tok_count = route_block.shape[0]
    ordered = jnp.transpose(route_block).reshape(-1)
    onehot = (ordered[:, None] == jnp.arange(experts, dtype=jnp.int32)[None, :]).astype(jnp.int32)
    before = jnp.cumsum(onehot, axis=0) - onehot
    position = jnp.sum(before * onehot, axis=1)
    return jnp.transpose(position.reshape(2, tok_count))


def linear(y, core, x, zh, b):
    return ((y * 2 + core) * (n_x * 2) + x * 2 + zh) * n_dp + b


def swap_pairs(flip, back):
    pairs = []
    for b in range(n_dp):
        for d in range(n_dp):
            for core in range(2):
                for x in range(n_x):
                    for zh in range(2):
                        at_batch = linear(d, core, x, zh, b)
                        at_part = linear((d - b) % n_dp, core, x, zh ^ flip, d)
                        pairs.append((at_part, at_batch) if back else (at_batch, at_part))
    return pairs


def swap(block, flip, back):
    return lax.ppermute(block, ("tensor", "expert", "dp"), swap_pairs(flip, back))


def shift_x(block, step):
    return lax.ppermute(
        block,
        "expert",
        [(x * 2 + zh, (x + step) % n_x * 2 + zh) for x in range(n_x) for zh in range(2)],
    )


def shift_y(block, step):
    return lax.ppermute(
        block,
        "tensor",
        [(y * 2 + core, (y + step) % n_y * 2 + core) for y in range(n_y) for core in range(2)],
    )


def other_core(block):
    return lax.ppermute(block, "tensor", [(t, t ^ 1) for t in range(2 * n_y)])


def shift(block, step):
    return lax.ppermute(block, "dp", [(i, i + step) for i in range(n_dp) if 0 <= i + step < n_dp])


def unit_kernel(where_ref, pre_ref, act_ref, out_ref):
    unit = act_ref[...].astype(f32) * gelu_slope(pre_ref[...].astype(f32))
    out_ref[...] = unit.astype(bf16)


def unit_of(pre, act, where, c, part):
    hidden = pre.shape[-1]
    block = (1, 1, part, hidden)
    taken = pl.BlockSpec(
        block, lambda kz, kx, w: (lax.rem(w[0] - kx + n_x, n_x), lax.rem(w[1] + kz, 2), c, 0)
    )
    size = 2 * n_x * part * hidden
    return pl.pallas_call(
        unit_kernel,
        grid_spec=pltpu.PrefetchScalarGridSpec(
            num_scalar_prefetch=1,
            grid=(2, n_x),
            in_specs=[taken, taken],
            out_specs=pl.BlockSpec(block, lambda kz, kx, w: (kz, kx, 0, 0)),
        ),
        out_shape=jax.ShapeDtypeStruct((2, n_x, part, hidden), bf16),
        cost_estimate=pl.CostEstimate(flops=16 * size, bytes_accessed=6 * size, transcendentals=size),
        compiler_params=pltpu.CompilerParams(vmem_limit_bytes=32 << 20),
    )(where, pre, act).reshape(2 * n_x * part, hidden)


def slot_kernel(rows, half, where_ref, *refs):
    own, right, left, weight = refs[0], refs[1:4], refs[4:7], refs[7]
    keep_ref, send_ref, unit, held, sems = refs[8:]
    place, y, core = where_ref[0], where_ref[1], where_ref[2]
    load_w = pltpu.make_async_copy(weight, held, sems.at[4])
    load_w.start()
    pltpu.make_async_copy(own, unit.at[0], sems.at[0]).start()
    for j in range(1, 4):

        @pl.when(place >= j)
        def _():
            pltpu.make_async_copy(right[j - 1], unit.at[j], sems.at[j]).start()

        @pl.when(place < j)
        def _():
            pltpu.make_async_copy(left[3 - j], unit.at[j], sems.at[j]).start()

    load_w.wait()
    kept = pl.multiple_of(core * half, half)
    sent = pl.multiple_of((1 - core) * half, half)
    for j in range(4):
        pltpu.make_async_copy(own, unit.at[j], sems.at[j]).wait()
        slot = lax.rem(j - y + n_y, n_y)
        for start, out in ((kept, keep_ref), (sent, send_ref)):
            out[slot] = lax.dot_general(
                unit[j],
                held[pl.ds(start, half), :],
                (((1,), (1,)), ((), ())),
                preferred_element_type=f32,
            ).astype(bf16)


def slot_part(own, right, left, weight, where):
    rows, hidden = own.shape
    width = weight.shape[0]
    half = width // 2
    anywhere = pl.BlockSpec(memory_space=pl.ANY)
    whole = pl.BlockSpec(memory_space=pltpu.VMEM)
    return pl.pallas_call(
        functools.partial(slot_kernel, rows, half),
        in_specs=[pl.BlockSpec(memory_space=pltpu.SMEM)] + [anywhere] * 8,
        out_specs=[whole, whole],
        out_shape=[jax.ShapeDtypeStruct((4, rows, half), bf16)] * 2,
        scratch_shapes=[
            pltpu.VMEM((4, rows, hidden), bf16),
            pltpu.VMEM((width, hidden), bf16),
            pltpu.SemaphoreType.DMA((5,)),
        ],
        cost_estimate=pl.CostEstimate(
            flops=8 * rows * hidden * width,
            bytes_accessed=2 * hidden * (4 * rows + width),
            transcendentals=0,
        ),
        compiler_params=pltpu.CompilerParams(vmem_limit_bytes=40 << 20),
    )(where, own, *right, *left, weight)


def grad_kernel(rows, half, where_ref, x_ref, *refs):
    out_ref = refs[-1]
    place = where_ref[0]
    totals = [None, None]
    for c in range(n_chunk):
        group = refs[7 * c : 7 * c + 7]
        for j in range(4):
            if j == 0:
                unit = group[0][...]
            else:
                unit = jnp.where(place >= j, group[j][...], group[7 - j][...])
            for h in range(2):
                term = jnp.dot(
                    x_ref[2 * j + h, :, c * rows : (c + 1) * rows], unit, preferred_element_type=f32
                )
                totals[h] = term if totals[h] is None else totals[h] + term
    for h in range(2):
        out_ref[h * half : (h + 1) * half, :] = totals[h].astype(bf16)


def grad_of(columns, units, where):
    half, all_rows = columns.shape[1:]
    rows = all_rows // n_chunk
    hidden = units[0].shape[1]
    tile = 256
    return pl.pallas_call(
        functools.partial(grad_kernel, rows, half),
        grid=(hidden // tile,),
        in_specs=[
            pl.BlockSpec(memory_space=pltpu.SMEM),
            pl.BlockSpec(columns.shape, lambda i: (0, 0, 0)),
        ]
        + [pl.BlockSpec((rows, tile), lambda i: (0, i))] * len(units),
        out_specs=pl.BlockSpec((2 * half, tile), lambda i: (0, i)),
        out_shape=jax.ShapeDtypeStruct((2 * half, hidden), bf16),
        cost_estimate=pl.CostEstimate(
            flops=16 * half * all_rows * hidden,
            bytes_accessed=2 * (columns.size + len(units) * rows * hidden + 2 * half * hidden),
            transcendentals=0,
        ),
        compiler_params=pltpu.CompilerParams(vmem_limit_bytes=40 << 20),
    )(where, columns, *units)


def per_device(tokens, routes, up_weight, saved_pre, grad_act):
    experts = lax.axis_size("expert")
    place = lax.axis_index("dp")
    tensor, expert = lax.axis_index("tensor"), lax.axis_index("expert")
    my_x, my_zh = expert // 2, expert % 2
    slot_count, hidden = saved_pre.shape[1:]
    capacity = slot_count // experts
    part = capacity // n_chunk
    tok_dev, width = tokens.shape
    weight = up_weight[0]
    pre = saved_pre.reshape(n_x, 2, capacity, hidden)
    act = grad_act.reshape(n_x, 2, capacity, hidden)
    group_at = jnp.stack([my_x, my_zh]).astype(jnp.int32)
    device_at = jnp.stack([place, tensor // 2, tensor % 2]).astype(jnp.int32)

    owns = [unit_of(pre, act, group_at, c, part) for c in range(n_chunk)]
    right, left = [[o] for o in owns], [[o] for o in owns]

    def step(c):
        right[c].append(shift(right[c][-1], 1))
        left[c].append(shift(left[c][-1], -1))

    for c in range(n_chunk):
        step(c)

    position = place_slots(routes, experts)
    kx = (routes // 2 - my_x) % n_x
    kz = (routes + my_zh) % 2
    row_of = (kz * n_x + kx) * capacity + position
    numbers = jnp.arange(slot_count, dtype=jnp.int32)
    holds = (row_of[:, 0, None] == numbers) | (row_of[:, 1, None] == numbers)
    outgoing = lax.dot_general(
        holds.astype(bf16), tokens, (((0,), (0,)), ((), ())), preferred_element_type=f32
    ).astype(bf16).reshape(2, n_x, capacity, width)
    outgoing, owns[0] = lax.optimization_barrier((outgoing, owns[0]))
    at_x = [outgoing[:, 0]] + [shift_x(outgoing[:, k], k) for k in range(1, n_x)]
    at_x = jnp.stack(at_x, axis=1)
    arrived = jnp.stack([swap(at_x[k], k, False) for k in range(2)])
    arrived = arrived.reshape(2 * n_x, n_chunk, part, width)
    arrived = jnp.transpose(arrived, (3, 1, 0, 2)).reshape(width, slot_count)
    columns = lax.all_gather(arrived, "tensor", axis=0, tiled=False)

    (right[0][1], left[0][1]), arrived = lax.optimization_barrier(
        ((right[0][1], left[0][1]), arrived)
    )
    step(0)
    step(1)
    step(0)
    step(1)

    returned = []
    for c in range(n_chunk):
        keep, send = slot_part(owns[c], right[c][1:], left[c][1:], weight, device_at)
        got = other_core(send)
        both = keep.astype(f32) + got.astype(f32)
        gathered = [shift_y(both[k].astype(bf16), k) for k in range(1, n_y)]
        summed = both[0]
        for block in gathered:
            summed = summed + block.astype(f32)
        summed = summed.astype(bf16).reshape(2, n_x * part, width)
        home = jnp.stack([swap(summed[k], k, True) for k in range(2)])
        home = home.reshape(2, n_x, part, width)
        at_home = [home[:, 0]] + [shift_x(home[:, k], -k) for k in range(1, n_x)]
        returned.append(jnp.stack(at_home, axis=1).reshape(2 * n_x * part, width))

    units = []
    for c in range(n_chunk):
        units += [owns[c]] + right[c][1:] + left[c][1:]
    grad_block = grad_of(columns, units, device_at)

    token_grad = jnp.zeros((tok_dev, width), f32)
    part_numbers = jnp.arange(2 * n_x * part, dtype=jnp.int32)
    row_in_part = (kz * n_x + kx) * part + position % part
    for c in range(n_chunk):
        row_c = jnp.where(position // part == c, row_in_part, -1)
        holds_c = (row_c[:, 0, None] == part_numbers) | (row_c[:, 1, None] == part_numbers)
        token_grad = token_grad + jnp.dot(
            holds_c.astype(bf16), returned[c], preferred_element_type=f32
        )
    return (token_grad.astype(bf16), grad_block[None])


def solution(mesh):
    placed = (
        P(("expert", "dp"), "tensor"),
        P(("expert", "dp"), None),
        P("expert", "dp", "tensor"),
        P("expert", "dp", "tensor"),
        P("expert", "dp", "tensor"),
    )
    return jax.shard_map(
        per_device,
        mesh=mesh,
        in_specs=placed,
        out_specs=(P(("expert", "dp"), "tensor"), P("expert", "dp", "tensor")),
        check_vma=False,
    )
```

time: 591 us -> 254 us (0.43)
  waiting for transfers between devices: 488 us -> 119 us
  starting transfers between devices: 19.5 us -> 78.3 us
  Pallas kernels: 0 us -> 29.8 us
  matrix products: 29 us -> 1.49 us
  blocking collectives: 14.3 us -> 0 us
  local copies, waits for them, and re-layouts: 14.4 us -> 8.29 us
  other arithmetic: 7.82 us -> 1.81 us
    all_gather x1, waiting for transfers between devices: 253 us -> 0.01 us  [per_device(): columns = lax.all_gather(arrived, 'tensor', axis=0, tiled=False)]
    reduce_scatter x1 -> x0, waiting for transfers between devices: 194 us -> none  [per_device(): lax.psum_scatter(lax.dot_general(arrived, unit_grad, (((0,), (0,)), ((),...]
    ppermute x0 -> x35, waiting for transfers between devices: none -> 119 us  [the longest x12 61.4 us: shift(): lax.ppermute(block, 'dp', [(i, i + step) for i in range(n_dp) if 0 <= i +...]
    ppermute x0 -> x35, starting transfers between devices: none -> 78.2 us  [the longest x12 41.3 us: shift(): lax.ppermute(block, 'dp', [(i, i + step) for i in range(n_dp) if 0 <= i +...]
    pallas_call x0 -> x5, Pallas kernels: none -> 29.8 us  [the longest x1 13 us: grad_of(): pl.pallas_call(functools.partial(grad_kernel, rows, half), grid=(hidden /...]
    dot_general x2 -> x3, matrix products: 29 us -> 1.49 us  [the longest x2 1.11 us: per_device(): jnp.dot(holds_c.astype(bf16), returned[c], preferred_element_type=f32)]
    unnamed x4 -> x1, waiting for transfers between devices: 26.5 us -> 0.02 us
    all_to_all x2 -> x0, starting transfers between devices: 19.2 us -> none  [the longest x1 9.61 us: per_device(): lax.all_to_all(summed, 'expert', split_axis=0, concat_axis=0, tiled=True)]
  transfers between devices with their start and end apart: 5 -> 36, of which waited for: 4 -> 16; matrix products, arithmetic and copies ran while one was open for 9% -> 3% of each run, Pallas kernels for 0% -> 6%
where the time goes in v2:
time: 254 us; the launch traced here: 253 us
  waiting for transfers between devices  119 us (47%)
  starting transfers between devices  78.3 us (31%)
  Pallas kernels  29.8 us (12%)
  between operations  14.6 us (6%)
  local copies, waits for them, and re-layouts  8.29 us (3%)
    ppermute x12, waiting for transfers between devices, shift(): lax.ppermute(block, 'dp', [(i, i + step) for i in range(n_dp) if 0 <= i +...  61.4 us
    ppermute x12, starting transfers between devices, shift(): lax.ppermute(block, 'dp', [(i, i + step) for i in range(n_dp) if 0 <= i +...  41.3 us
    ppermute x6, waiting for transfers between devices, swap(): lax.ppermute(block, ('tensor', 'expert', 'dp'), swap_pairs(flip, back))  31.8 us
    ppermute x6, starting transfers between devices, shift_y(): lax.ppermute(block, 'tensor', [(y * 2 + core, (y + step) % n_y * 2 + core...  15.9 us
    ppermute x9, waiting for transfers between devices, shift_x(): lax.ppermute(block, 'expert', [(x * 2 + zh, (x + step) % n_x * 2 + zh) fo...  14.5 us
    pallas_call x1, Pallas kernels, grad_of(): pl.pallas_call(functools.partial(grad_kernel, rows, half), grid=(hidden /...  13 us
    pallas_call x2, Pallas kernels, slot_part(): pl.pallas_call(functools.partial(slot_kernel, rows, half), in_specs=[pl.B...  12.3 us
    ppermute x6, starting transfers between devices, swap(): lax.ppermute(block, ('tensor', 'expert', 'dp'), swap_pairs(flip, back))  12.3 us
  transfers between devices with their start and end apart: 36, of which 16 were waited for; matrix products, arithmetic and copies ran while one was open for 3% of the time, Pallas kernels for 6%

profile of v2, /device:TPU:166, one launch (start us, length us, event | category | flops | bytes accessed | tf_op | source)
XLA Modules:
  0.0 253.0 jit_solution(5547575117102564407)
XLA Ops:
  7.3 1.6 copy-done.1
  8.9 1.6 copy-done.2
  10.5 2.2 shard_map.68
  12.8 2.9 %collective-permute-start.1 = (bf16[256,2048]{1,0:T(8,128)(2,1)S(1)}, bf16[256,2048]{1,0:T(8,128)(2,1)S(1)}, u32[]{:S(2)}, u32[]{:S(2)}) collective-permute-start(bf16[256,2048]{1,0:T(8,128)(2,1)S(1)} %bitcast.166), channel_id=1, source_target_pairs={{1,0},{2,1},{3,2},{5,4},{6,5},{7,6},{9,8},{10,9},{11,10},{13,12},{... | collective-permute-start | bytes 3145736 | tf_op jit(solution)/shard_map/ppermute | solution.py:76
  15.7 2.9 %collective-permute-start = (bf16[256,2048]{1,0:T(8,128)(2,1)S(1)}, bf16[256,2048]{1,0:T(8,128)(2,1)}, u32[]{:S(2)}, u32[]{:S(2)}) collective-permute-start(bf16[256,2048]{1,0:T(8,128)(2,1)S(1)} %bitcast.167), channel_id=1, source_target_pairs={{0,1},{1,2},{2,3},{4,5},{5,6},{6,7},{8,9},{9,10},{10,11},{12,13},{... | collective-permute-start | bytes 3145736 | tf_op jit(solution)/shard_map/ppermute | solution.py:76
  18.6 2.2 shard_map.70
  20.9 3.9 %collective-permute-start.18 = (bf16[256,2048]{1,0:T(8,128)(2,1)S(1)}, bf16[256,2048]{1,0:T(8,128)(2,1)}, u32[]{:S(2)}, u32[]{:S(2)}) collective-permute-start(bf16[256,2048]{1,0:T(8,128)(2,1)S(1)} %bitcast.170), channel_id=1, source_target_pairs={{1,0},{2,1},{3,2},{5,4},{6,5},{7,6},{9,8},{10,9},{11,10},{13,12},{... | collective-permute-start | bytes 3145736 | tf_op jit(solution)/shard_map/ppermute | solution.py:76
  24.8 1.9 collective-permute-start.15
  26.8 0.6 reduce-window.6
  27.4 0.2 slice_reduce_fusion
  27.8 0.4 convolution_convert_fusion
  28.2 0.6 collective-permute-start.30
  28.8 4.1 %collective-permute-done.30 = bf16[2,64,384]{2,1,0:T(8,128)(2,1)S(1)} collective-permute-done((bf16[2,64,384]{2,1,0:T(8,128)(2,1)S(1)}, bf16[2,64,384]{2,1,0:T(8,128)(2,1)S(1)}, u32[]{:S(2)}, u32[]{:S(2)}) %collective-permute-start.30) | collective-permute-done | bytes 98336 | tf_op jit(solution)/shard_map/ppermute | solution.py:56
  32.9 0.8 collective-permute-start.32
  33.7 5.0 %collective-permute-done.32 = bf16[2,64,384]{2,1,0:T(8,128)(2,1)S(1)} collective-permute-done((bf16[2,64,384]{2,1,0:T(8,128)(2,1)S(1)}, bf16[2,64,384]{2,1,0:T(8,128)(2,1)S(1)}, u32[]{:S(2)}, u32[]{:S(2)}) %collective-permute-start.32) | collective-permute-done | bytes 98336 | tf_op jit(solution)/shard_map/ppermute | solution.py:56
  38.7 0.2 collective-permute-start.31
  38.9 23.2 %collective-permute-done.18.refs_4_.refs_11_ = bf16[256,2048]{1,0:T(8,128)(2,1)} collective-permute-done((bf16[256,2048]{1,0:T(8,128)(2,1)S(1)}, bf16[256,2048]{1,0:T(8,128)(2,1)}, u32[]{:S(2)}, u32[]{:S(2)}) %collective-permute-start.18) | collective-permute-done | bytes 1048608 | tf_op jit(solution)/shard_map/ppermute | solution.py:76
  62.1 2.9 %collective-permute-start.19 = (bf16[256,2048]{1,0:T(8,128)(2,1)}, bf16[256,2048]{1,0:T(8,128)(2,1)}, u32[]{:S(2)}, u32[]{:S(2)}) collective-permute-start(bf16[256,2048]{1,0:T(8,128)(2,1)} %collective-permute-done.18.refs_4_.refs_11_), channel_id=1, source_target_pairs={{1,0},{2,1},{3,2},{5,4},{6,5},{7,6},{9,8},{10,9},{11,10},{13,12},{... | collective-permute-start | bytes 3145736 | tf_op jit(solution)/shard_map/ppermute | solution.py:76
  65.1 2.9 %collective-permute-start.16 = (bf16[256,2048]{1,0:T(8,128)(2,1)}, bf16[256,2048]{1,0:T(8,128)(2,1)}, u32[]{:S(2)}, u32[]{:S(2)}) collective-permute-start(bf16[256,2048]{1,0:T(8,128)(2,1)} %collective-permute-done.15.refs_1_.refs_8_), channel_id=1, source_target_pairs={{0,1},{1,2},{2,3},{4,5},{5,6},{6,7},{8,9},{9,10},{10,11},{12,13},{... | collective-permute-start | bytes 3145736 | tf_op jit(solution)/shard_map/ppermute | solution.py:76
  68.1 6.4 %collective-permute-start.33 = (bf16[4,64,384]{2,1,0:T(8,128)(2,1)S(1)}, bf16[4,64,384]{2,1,0:T(8,128)(2,1)S(1)}, u32[]{:S(2)}, u32[]{:S(2)}) collective-permute-start(bf16[4,64,384]{2,1,0:T(8,128)(2,1)S(1)} %get-tuple-element.30), channel_id=1, source_target_pairs={{0,0},{4,4},{8,8},{12,12},{16,16},{20,20},{24,24},{28,28},{32,32},... | collective-permute-start | bytes 589832 | tf_op jit(solution)/shard_map/ppermute | solution.py:52
  74.6 3.6 %collective-permute-start.2 = (bf16[256,2048]{1,0:T(8,128)(2,1)}, bf16[256,2048]{1,0:T(8,128)(2,1)}, u32[]{:S(2)}, u32[]{:S(2)}) collective-permute-start(bf16[256,2048]{1,0:T(8,128)(2,1)} %collective-permute-done.refs_1_), channel_id=1, source_target_pairs={{0,1},{1,2},{2,3},{4,5},{5,6},{6,7},{8,9},{9,10},{10,11},{12,13},{... | collective-permute-start | bytes 3145736 | tf_op jit(solution)/shard_map/ppermute | solution.py:76
  78.2 21.8 %collective-permute-done.33 = bf16[4,64,384]{2,1,0:T(8,128)(2,1)S(1)} collective-permute-done((bf16[4,64,384]{2,1,0:T(8,128)(2,1)S(1)}, bf16[4,64,384]{2,1,0:T(8,128)(2,1)S(1)}, u32[]{:S(2)}, u32[]{:S(2)}) %collective-permute-start.33) | collective-permute-done | bytes 196640 | tf_op jit(solution)/shard_map/ppermute | solution.py:52
  100.0 1.9 collective-permute-start.4
  102.0 0.8 copy.45
  102.8 1.9 copy.46
  104.7 1.9 collective-permute-start.20
  106.7 6.4 %collective-permute-start.17 = (bf16[256,2048]{1,0:T(8,128)(2,1)}, bf16[256,2048]{1,0:T(8,128)(2,1)}, u32[]{:S(2)}, u32[]{:S(2)}) collective-permute-start(bf16[256,2048]{1,0:T(8,128)(2,1)} %collective-permute-done.16.refs_2_.refs_9_), channel_id=1, source_target_pairs={{0,1},{1,2},{2,3},{4,5},{5,6},{6,7},{8,9},{9,10},{10,11},{12,13},{... | collective-permute-start | bytes 3145736 | tf_op jit(solution)/shard_map/ppermute | solution.py:76
  113.1 9.7 %collective-permute-done.2.refs_2_ = bf16[256,2048]{1,0:T(8,128)(2,1)} collective-permute-done((bf16[256,2048]{1,0:T(8,128)(2,1)}, bf16[256,2048]{1,0:T(8,128)(2,1)}, u32[]{:S(2)}, u32[]{:S(2)}) %collective-permute-start.2) | collective-permute-done | bytes 1048608 | tf_op jit(solution)/shard_map/ppermute | solution.py:76
  122.8 8.1 %collective-permute-start.3 = (bf16[256,2048]{1,0:T(8,128)(2,1)}, bf16[256,2048]{1,0:T(8,128)(2,1)}, u32[]{:S(2)}, u32[]{:S(2)}) collective-permute-start(bf16[256,2048]{1,0:T(8,128)(2,1)} %collective-permute-done.2.refs_2_), channel_id=1, source_target_pairs={{0,1},{1,2},{2,3},{4,5},{5,6},{6,7},{8,9},{9,10},{10,11},{12,13},{... | collective-permute-start | bytes 3145736 | tf_op jit(solution)/shard_map/ppermute | solution.py:76
  130.9 1.9 collective-permute-start.5
  132.9 17.6 %collective-permute-done.20.refs_6_.refs_13_ = bf16[256,2048]{1,0:T(8,128)(2,1)} collective-permute-done((bf16[256,2048]{1,0:T(8,128)(2,1)}, bf16[256,2048]{1,0:T(8,128)(2,1)}, u32[]{:S(2)}, u32[]{:S(2)}) %collective-permute-start.20) | collective-permute-done | bytes 1048608 | tf_op jit(solution)/shard_map/ppermute | solution.py:76
  150.6 1.9 copy-done.3
  152.5 6.0 %shard_map.71 = (bf16[4,256,384]{2,1,0:T(8,128)(2,1)S(1)}, bf16[4,256,384]{2,1,0:T(8,128)(2,1)S(1)}) custom-call(s32[3]{0:T(128)S(1)} %pad_add_fusion.where_ref, bf16[256,2048]{1,0:T(8,128)(2,1)S(1)} %bitcast.172, bf16[256,2048]{1,0:T(8,128)(2,1)} %collective-permute-done.15.refs_1_.refs_8_, bf16[256,2048]{1,0:T(8,128)(2,1)} %collective-permute-done.16.refs_2_.refs_9_, ...), custom_call_target="tpu_custom_call" | custom-call | flops 3221225472 | bytes 7340032 | tf_op jit(solution)/shard_map/pallas_call | solution.py:143
  158.6 6.8 %collective-permute-done.3.refs_3_ = bf16[256,2048]{1,0:T(8,128)(2,1)} collective-permute-done((bf16[256,2048]{1,0:T(8,128)(2,1)}, bf16[256,2048]{1,0:T(8,128)(2,1)}, u32[]{:S(2)}, u32[]{:S(2)}) %collective-permute-start.3) | collective-permute-done | bytes 1048608 | tf_op jit(solution)/shard_map/ppermute | solution.py:76
  165.4 4.1 %collective-permute-done.5.refs_6_ = bf16[256,2048]{1,0:T(8,128)(2,1)} collective-permute-done((bf16[256,2048]{1,0:T(8,128)(2,1)}, bf16[256,2048]{1,0:T(8,128)(2,1)}, u32[]{:S(2)}, u32[]{:S(2)}) %collective-permute-start.5) | collective-permute-done | bytes 1048608 | tf_op jit(solution)/shard_map/ppermute | solution.py:76
  169.5 6.2 %shard_map.69 = (bf16[4,256,384]{2,1,0:T(8,128)(2,1)S(1)}, bf16[4,256,384]{2,1,0:T(8,128)(2,1)S(1)}) custom-call(s32[3]{0:T(128)S(1)} %pad_add_fusion.where_ref, bf16[256,2048]{1,0:T(8,128)(2,1)S(1)} %bitcast.168, bf16[256,2048]{1,0:T(8,128)(2,1)} %collective-permute-done.refs_1_, bf16[256,2048]{1,0:T(8,128)(2,1)} %collective-permute-done.2.refs_2_, ...), custom_call_target="tpu_custom_call" | custom-call | flops 3221225472 | bytes 7340032 | tf_op jit(solution)/shard_map/pallas_call | solution.py:143
  175.8 0.2 fusion.45
  176.1 8.8 %collective-permute-start.22 = (bf16[256,384]{1,0:T(8,128)(2,1)S(1)}, bf16[256,384]{1,0:T(8,128)(2,1)S(1)}, u32[]{:S(2)}, u32[]{:S(2)}) collective-permute-start(bf16[256,384]{1,0:T(8,128)(2,1)S(1)} %get-tuple-element.27), channel_id=1, source_target_pairs={{0,64},{32,96},{64,128},{96,160},{128,192},{160,224},{192,0},{224,... | collective-permute-start | bytes 589832 | tf_op jit(solution)/shard_map/ppermute | solution.py:64
  184.9 0.8 collective-permute-start.24
  185.7 1.4 collective-permute-start.23
  187.1 0.2 fusion.44
  187.4 1.5 collective-permute-start.7
  188.9 1.8 collective-permute-start.9
  190.7 0.4 collective-permute-done.22
  191.1 1.6 collective-permute-start.8
  192.7 4.2 %collective-permute-done.23 = bf16[256,384]{1,0:T(8,128)(2,1)S(1)} collective-permute-done((bf16[256,384]{1,0:T(8,128)(2,1)S(1)}, bf16[256,384]{1,0:T(8,128)(2,1)S(1)}, u32[]{:S(2)}, u32[]{:S(2)}) %collective-permute-start.23) | collective-permute-done | bytes 196640 | tf_op jit(solution)/shard_map/ppermute | solution.py:64
  197.1 3.4 %collective-permute-start.25 = (bf16[128,384]{1,0:T(8,128)(2,1)S(1)}, bf16[128,384]{1,0:T(8,128)(2,1)S(1)}, u32[]{:S(2)}, u32[]{:S(2)}) collective-permute-start(bf16[128,384]{1,0:T(8,128)(2,1)S(1)} %get-tuple-element.45), channel_id=1, source_target_pairs={{0,0},{4,4},{8,8},{12,12},{16,16},{20,20},{24,24},{28,28},{32,32},... | collective-permute-start | bytes 294920 | tf_op jit(solution)/shard_map/ppermute | solution.py:52
  200.6 0.5 collective-permute-done.9
  201.1 5.9 %collective-permute-done.8 = bf16[256,384]{1,0:T(8,128)(2,1)S(1)} collective-permute-done((bf16[256,384]{1,0:T(8,128)(2,1)S(1)}, bf16[256,384]{1,0:T(8,128)(2,1)S(1)}, u32[]{:S(2)}, u32[]{:S(2)}) %collective-permute-start.8) | collective-permute-done | bytes 196640 | tf_op jit(solution)/shard_map/ppermute | solution.py:64
  207.2 1.9 collective-permute-start.10
  209.1 0.5 collective-permute-start.11
  209.5 3.5 %collective-permute-done.26 = bf16[128,384]{1,0:T(8,128)(2,1)S(1)} collective-permute-done((bf16[128,384]{1,0:T(8,128)(2,1)S(1)}, bf16[128,384]{1,0:T(8,128)(2,1)S(1)}, u32[]{:S(2)}, u32[]{:S(2)}) %collective-permute-start.26) | collective-permute-done | bytes 98336 | tf_op jit(solution)/shard_map/ppermute | solution.py:52
  213.0 0.9 collective-permute-start.27
  214.0 2.4 collective-permute-start.29
  216.4 0.2 collective-permute-start.28
  216.6 6.4 %collective-permute-done.11 = bf16[128,384]{1,0:T(8,128)(2,1)S(1)} collective-permute-done((bf16[128,384]{1,0:T(8,128)(2,1)S(1)}, bf16[128,384]{1,0:T(8,128)(2,1)S(1)}, u32[]{:S(2)}, u32[]{:S(2)}) %collective-permute-start.11) | collective-permute-done | bytes 98336 | tf_op jit(solution)/shard_map/ppermute | solution.py:52
  223.1 0.9 collective-permute-start.12
  224.0 2.4 collective-permute-start.14
  226.4 0.2 collective-permute-start.13
  226.6 1.8 collective-permute-done.12
  228.4 3.5 %collective-permute-done.13 = bf16[2,32,384]{2,1,0:T(8,128)(2,1)S(1)} collective-permute-done((bf16[2,32,384]{2,1,0:T(8,128)(2,1)S(1)}, bf16[2,32,384]{2,1,0:T(8,128)(2,1)S(1)}, u32[]{:S(2)}, u32[]{:S(2)}) %collective-permute-start.13) | collective-permute-done | bytes 49184 | tf_op jit(solution)/shard_map/ppermute | solution.py:56
  232.0 0.2 fusion.16
  232.2 0.9 fusion
  233.1 13.0 %shard_map.72 = bf16[768,2048]{1,0:T(8,128)(2,1)} custom-call(s32[3]{0:T(128)S(1)} %pad_add_fusion.where_ref, bf16[8,384,512]{2,1,0:T(8,128)(2,1)} %all-gather.2.cloned.1.call-done.x_ref, bf16[256,2048]{1,0:T(8,128)(2,1)S(1)} %bitcast.169, bf16[256,2048]{1,0:T(8,128)(2,1)} %collective-permute-done.refs_1_, bf16[256,2048]{1,0:T(8,128)(2,1)} %collective-permute-done.2.refs_2_, ...), custom_call_target="tpu_custom_call" | custom-call | flops 6442450944 | bytes 20971520 | tf_op jit(solution)/shard_map/pallas_call | solution.py:187
  (61 shorter events, 1.5 us)
Async XLA Ops:
  7.2 20.6 %copy-start = (bf16[128,384]{1,0:T(8,128)(2,1)S(1)}, bf16[128,384]{1,0:T(8,128)(2,1)}, u32[]{:S(2)}) copy-start(bf16[128,384]{1,0:T(8,128)(2,1)} %param.5) | copy-start | bytes 294916
  7.2 225.9 %all-gather.2.cloned.1.call-start = ((), (), s32[]{:S(2)}) async-start(), calls=%async_computation | async-start | bytes 3538944 | tf_op jit(solution)/shard_map/all_gather | solution.py:246
  7.3 1.6 copy-start.1
  8.9 1.6 copy-start.2
  12.8 14.0 %copy-start.5 = (s32[128,2]{0,1:T(2,128)S(1)}, s32[128,2]{0,1:T(2,128)}, u32[]{:S(2)}) copy-start(s32[128,2]{0,1:T(2,128)} %param.6) | copy-start | bytes 3076
  12.8 61.7 %collective-permute-start.1 = (bf16[256,2048]{1,0:T(8,128)(2,1)S(1)}, bf16[256,2048]{1,0:T(8,128)(2,1)S(1)}, u32[]{:S(2)}, u32[]{:S(2)}) collective-permute-start(bf16[256,2048]{1,0:T(8,128)(2,1)S(1)} %bitcast.166), channel_id=1, source_target_pairs={{1,0},{2,1},{3,2},{5,4},{6,5},{7,6},{9,8},{10,9},{11,10},{13,12},{... | collective-permute-start | bytes 3145736 | tf_op jit(solution)/shard_map/ppermute | solution.py:76
  15.7 58.9 %collective-permute-start = (bf16[256,2048]{1,0:T(8,128)(2,1)S(1)}, bf16[256,2048]{1,0:T(8,128)(2,1)}, u32[]{:S(2)}, u32[]{:S(2)}) collective-permute-start(bf16[256,2048]{1,0:T(8,128)(2,1)S(1)} %bitcast.167), channel_id=1, source_target_pairs={{0,1},{1,2},{2,3},{4,5},{5,6},{6,7},{8,9},{9,10},{10,11},{12,13},{... | collective-permute-start | bytes 3145736 | tf_op jit(solution)/shard_map/ppermute | solution.py:76
  20.9 41.3 %collective-permute-start.18 = (bf16[256,2048]{1,0:T(8,128)(2,1)S(1)}, bf16[256,2048]{1,0:T(8,128)(2,1)}, u32[]{:S(2)}, u32[]{:S(2)}) collective-permute-start(bf16[256,2048]{1,0:T(8,128)(2,1)S(1)} %bitcast.170), channel_id=1, source_target_pairs={{1,0},{2,1},{3,2},{5,4},{6,5},{7,6},{9,8},{10,9},{11,10},{13,12},{... | collective-permute-start | bytes 3145736 | tf_op jit(solution)/shard_map/ppermute | solution.py:76
  24.8 40.2 %collective-permute-start.15 = (bf16[256,2048]{1,0:T(8,128)(2,1)S(1)}, bf16[256,2048]{1,0:T(8,128)(2,1)}, u32[]{:S(2)}, u32[]{:S(2)}) collective-permute-start(bf16[256,2048]{1,0:T(8,128)(2,1)S(1)} %bitcast.171), channel_id=1, source_target_pairs={{0,1},{1,2},{2,3},{4,5},{5,6},{6,7},{8,9},{9,10},{10,11},{12,13},{... | collective-permute-start | bytes 3145736 | tf_op jit(solution)/shard_map/ppermute | solution.py:76
  28.2 4.7 %collective-permute-start.30 = (bf16[2,64,384]{2,1,0:T(8,128)(2,1)S(1)}, bf16[2,64,384]{2,1,0:T(8,128)(2,1)S(1)}, u32[]{:S(2)}, u32[]{:S(2)}) collective-permute-start(bf16[2,64,384]{2,1,0:T(8,128)(2,1)S(1)} %get-tuple-element.32), channel_id=1, source_target_pairs={{0,8},{4,12},{8,16},{12,20},{16,24},{20,28},{24,0},{28,4},{1,9},{5... | collective-permute-start | bytes 294920 | tf_op jit(solution)/shard_map/ppermute | solution.py:56
  32.9 5.8 %collective-permute-start.32 = (bf16[2,64,384]{2,1,0:T(8,128)(2,1)S(1)}, bf16[2,64,384]{2,1,0:T(8,128)(2,1)S(1)}, u32[]{:S(2)}, u32[]{:S(2)}) collective-permute-start(bf16[2,64,384]{2,1,0:T(8,128)(2,1)S(1)} %get-tuple-element.33), channel_id=1, source_target_pairs={{0,24},{4,28},{8,0},{12,4},{16,8},{20,12},{24,16},{28,20},{1,25},{... | collective-permute-start | bytes 294920 | tf_op jit(solution)/shard_map/ppermute | solution.py:56
  38.7 29.3 %collective-permute-start.31 = (bf16[2,64,384]{2,1,0:T(8,128)(2,1)S(1)}, bf16[2,64,384]{2,1,0:T(8,128)(2,1)S(1)}, u32[]{:S(2)}, u32[]{:S(2)}) collective-permute-start(bf16[2,64,384]{2,1,0:T(8,128)(2,1)S(1)} %get-tuple-element.34), channel_id=1, source_target_pairs={{0,16},{4,20},{8,24},{12,28},{16,0},{20,4},{24,8},{28,12},{1,17},{... | collective-permute-start | bytes 294920 | tf_op jit(solution)/shard_map/ppermute | solution.py:56
  62.1 42.6 %collective-permute-start.19 = (bf16[256,2048]{1,0:T(8,128)(2,1)}, bf16[256,2048]{1,0:T(8,128)(2,1)}, u32[]{:S(2)}, u32[]{:S(2)}) collective-permute-start(bf16[256,2048]{1,0:T(8,128)(2,1)} %collective-permute-done.18.refs_4_.refs_11_), channel_id=1, source_target_pairs={{1,0},{2,1},{3,2},{5,4},{6,5},{7,6},{9,8},{10,9},{11,10},{13,12},{... | collective-permute-start | bytes 3145736 | tf_op jit(solution)/shard_map/ppermute | solution.py:76
  65.1 41.6 %collective-permute-start.16 = (bf16[256,2048]{1,0:T(8,128)(2,1)}, bf16[256,2048]{1,0:T(8,128)(2,1)}, u32[]{:S(2)}, u32[]{:S(2)}) collective-permute-start(bf16[256,2048]{1,0:T(8,128)(2,1)} %collective-permute-done.15.refs_1_.refs_8_), channel_id=1, source_target_pairs={{0,1},{1,2},{2,3},{4,5},{5,6},{6,7},{8,9},{9,10},{10,11},{12,13},{... | collective-permute-start | bytes 3145736 | tf_op jit(solution)/shard_map/ppermute | solution.py:76
  68.1 31.9 %collective-permute-start.33 = (bf16[4,64,384]{2,1,0:T(8,128)(2,1)S(1)}, bf16[4,64,384]{2,1,0:T(8,128)(2,1)S(1)}, u32[]{:S(2)}, u32[]{:S(2)}) collective-permute-start(bf16[4,64,384]{2,1,0:T(8,128)(2,1)S(1)} %get-tuple-element.30), channel_id=1, source_target_pairs={{0,0},{4,4},{8,8},{12,12},{16,16},{20,20},{24,24},{28,28},{32,32},... | collective-permute-start | bytes 589832 | tf_op jit(solution)/shard_map/ppermute | solution.py:52
  74.5 27.4 %collective-permute-start.34 = (bf16[4,64,384]{2,1,0:T(8,128)(2,1)S(1)}, bf16[4,64,384]{2,1,0:T(8,128)(2,1)S(1)}, u32[]{:S(2)}, u32[]{:S(2)}) collective-permute-start(bf16[4,64,384]{2,1,0:T(8,128)(2,1)S(1)} %get-tuple-element.31), channel_id=1, source_target_pairs={{0,4},{4,0},{8,12},{12,8},{16,20},{20,16},{24,28},{28,24},{32,36},... | collective-permute-start | bytes 589832 | tf_op jit(solution)/shard_map/ppermute | solution.py:52
  74.6 48.2 %collective-permute-start.2 = (bf16[256,2048]{1,0:T(8,128)(2,1)}, bf16[256,2048]{1,0:T(8,128)(2,1)}, u32[]{:S(2)}, u32[]{:S(2)}) collective-permute-start(bf16[256,2048]{1,0:T(8,128)(2,1)} %collective-permute-done.refs_1_), channel_id=1, source_target_pairs={{0,1},{1,2},{2,3},{4,5},{5,6},{6,7},{8,9},{9,10},{10,11},{12,13},{... | collective-permute-start | bytes 3145736 | tf_op jit(solution)/shard_map/ppermute | solution.py:76
  100.0 30.9 %collective-permute-start.4 = (bf16[256,2048]{1,0:T(8,128)(2,1)S(1)}, bf16[256,2048]{1,0:T(8,128)(2,1)}, u32[]{:S(2)}, u32[]{:S(2)}) collective-permute-start(bf16[256,2048]{1,0:T(8,128)(2,1)S(1)} %collective-permute-done.1.refs_4_), channel_id=1, source_target_pairs={{1,0},{2,1},{3,2},{5,4},{6,5},{7,6},{9,8},{10,9},{11,10},{13,12},{... | collective-permute-start | bytes 3145736 | tf_op jit(solution)/shard_map/ppermute | solution.py:76
  104.7 45.8 %collective-permute-start.20 = (bf16[256,2048]{1,0:T(8,128)(2,1)}, bf16[256,2048]{1,0:T(8,128)(2,1)}, u32[]{:S(2)}, u32[]{:S(2)}) collective-permute-start(bf16[256,2048]{1,0:T(8,128)(2,1)} %collective-permute-done.19.refs_5_.refs_12_), channel_id=1, source_target_pairs={{1,0},{2,1},{3,2},{5,4},{6,5},{7,6},{9,8},{10,9},{11,10},{13,12},{... | collective-permute-start | bytes 3145736 | tf_op jit(solution)/shard_map/ppermute | solution.py:76
  106.7 43.9 %collective-permute-start.17 = (bf16[256,2048]{1,0:T(8,128)(2,1)}, bf16[256,2048]{1,0:T(8,128)(2,1)}, u32[]{:S(2)}, u32[]{:S(2)}) collective-permute-start(bf16[256,2048]{1,0:T(8,128)(2,1)} %collective-permute-done.16.refs_2_.refs_9_), channel_id=1, source_target_pairs={{0,1},{1,2},{2,3},{4,5},{5,6},{6,7},{8,9},{9,10},{10,11},{12,13},{... | collective-permute-start | bytes 3145736 | tf_op jit(solution)/shard_map/ppermute | solution.py:76
  122.8 42.6 %collective-permute-start.3 = (bf16[256,2048]{1,0:T(8,128)(2,1)}, bf16[256,2048]{1,0:T(8,128)(2,1)}, u32[]{:S(2)}, u32[]{:S(2)}) collective-permute-start(bf16[256,2048]{1,0:T(8,128)(2,1)} %collective-permute-done.2.refs_2_), channel_id=1, source_target_pairs={{0,1},{1,2},{2,3},{4,5},{5,6},{6,7},{8,9},{9,10},{10,11},{12,13},{... | collective-permute-start | bytes 3145736 | tf_op jit(solution)/shard_map/ppermute | solution.py:76
  130.9 38.6 %collective-permute-start.5 = (bf16[256,2048]{1,0:T(8,128)(2,1)}, bf16[256,2048]{1,0:T(8,128)(2,1)}, u32[]{:S(2)}, u32[]{:S(2)}) collective-permute-start(bf16[256,2048]{1,0:T(8,128)(2,1)} %collective-permute-done.4.refs_5_), channel_id=1, source_target_pairs={{1,0},{2,1},{3,2},{5,4},{6,5},{7,6},{9,8},{10,9},{11,10},{13,12},{... | collective-permute-start | bytes 3145736 | tf_op jit(solution)/shard_map/ppermute | solution.py:76
  150.6 1.9 copy-start.3
  152.5 17.0 %copy-start.4 = (bf16[1,768,2048]{2,1,0:T(8,128)(2,1)S(1)}, bf16[1,768,2048]{2,1,0:T(8,128)(2,1)}, u32[]{:S(2)}) copy-start(bf16[1,768,2048]{2,1,0:T(8,128)(2,1)} %param.7) | copy-start | bytes 9437188
  158.5 17.3 %collective-permute-start.21 = (bf16[4,256,384]{2,1,0:T(8,128)(2,1)S(1)}, bf16[4,256,384]{2,1,0:T(8,128)(2,1)S(1)}, u32[]{:S(2)}, u32[]{:S(2)}) collective-permute-start(bf16[4,256,384]{2,1,0:T(8,128)(2,1)S(1)} %get-tuple-element.16), channel_id=1, source_target_pairs={{0,32},{32,0},{64,96},{96,64},{128,160},{160,128},{192,224},{224,1... | collective-permute-start | bytes 2359304 | tf_op jit(solution)/shard_map/ppermute | solution.py:72
  175.7 11.4 %collective-permute-start.6 = (bf16[4,256,384]{2,1,0:T(8,128)(2,1)S(1)}, bf16[4,256,384]{2,1,0:T(8,128)(2,1)S(1)}, u32[]{:S(2)}, u32[]{:S(2)}) collective-permute-start(bf16[4,256,384]{2,1,0:T(8,128)(2,1)S(1)} %get-tuple-element.14), channel_id=1, source_target_pairs={{0,32},{32,0},{64,96},{96,64},{128,160},{160,128},{192,224},{224,1... | collective-permute-start | bytes 2359304 | tf_op jit(solution)/shard_map/ppermute | solution.py:72
  176.1 15.0 %collective-permute-start.22 = (bf16[256,384]{1,0:T(8,128)(2,1)S(1)}, bf16[256,384]{1,0:T(8,128)(2,1)S(1)}, u32[]{:S(2)}, u32[]{:S(2)}) collective-permute-start(bf16[256,384]{1,0:T(8,128)(2,1)S(1)} %get-tuple-element.27), channel_id=1, source_target_pairs={{0,64},{32,96},{64,128},{96,160},{128,192},{160,224},{192,0},{224,... | collective-permute-start | bytes 589832 | tf_op jit(solution)/shard_map/ppermute | solution.py:64
  184.9 7.8 %collective-permute-start.24 = (bf16[256,384]{1,0:T(8,128)(2,1)S(1)}, bf16[256,384]{1,0:T(8,128)(2,1)S(1)}, u32[]{:S(2)}, u32[]{:S(2)}) collective-permute-start(bf16[256,384]{1,0:T(8,128)(2,1)S(1)} %get-tuple-element.28), channel_id=1, source_target_pairs={{0,192},{32,224},{64,0},{96,32},{128,64},{160,96},{192,128},{224,1... | collective-permute-start | bytes 589832 | tf_op jit(solution)/shard_map/ppermute | solution.py:64
  185.7 11.3 %collective-permute-start.23 = (bf16[256,384]{1,0:T(8,128)(2,1)S(1)}, bf16[256,384]{1,0:T(8,128)(2,1)S(1)}, u32[]{:S(2)}, u32[]{:S(2)}) collective-permute-start(bf16[256,384]{1,0:T(8,128)(2,1)S(1)} %get-tuple-element.29), channel_id=1, source_target_pairs={{0,128},{32,160},{64,192},{96,224},{128,0},{160,32},{192,64},{224,... | collective-permute-start | bytes 589832 | tf_op jit(solution)/shard_map/ppermute | solution.py:64
  187.4 13.2 %collective-permute-start.7 = (bf16[256,384]{1,0:T(8,128)(2,1)S(1)}, bf16[256,384]{1,0:T(8,128)(2,1)S(1)}, u32[]{:S(2)}, u32[]{:S(2)}) collective-permute-start(bf16[256,384]{1,0:T(8,128)(2,1)S(1)} %get-tuple-element.24), channel_id=1, source_target_pairs={{0,64},{32,96},{64,128},{96,160},{128,192},{160,224},{192,0},{224,... | collective-permute-start | bytes 589832 | tf_op jit(solution)/shard_map/ppermute | solution.py:64
  188.9 12.3 %collective-permute-start.9 = (bf16[256,384]{1,0:T(8,128)(2,1)S(1)}, bf16[256,384]{1,0:T(8,128)(2,1)S(1)}, u32[]{:S(2)}, u32[]{:S(2)}) collective-permute-start(bf16[256,384]{1,0:T(8,128)(2,1)S(1)} %get-tuple-element.25), channel_id=1, source_target_pairs={{0,192},{32,224},{64,0},{96,32},{128,64},{160,96},{192,128},{224,1... | collective-permute-start | bytes 589832 | tf_op jit(solution)/shard_map/ppermute | solution.py:64
  191.1 15.9 %collective-permute-start.8 = (bf16[256,384]{1,0:T(8,128)(2,1)S(1)}, bf16[256,384]{1,0:T(8,128)(2,1)S(1)}, u32[]{:S(2)}, u32[]{:S(2)}) collective-permute-start(bf16[256,384]{1,0:T(8,128)(2,1)S(1)} %get-tuple-element.26), channel_id=1, source_target_pairs={{0,128},{32,160},{64,192},{96,224},{128,0},{160,32},{192,64},{224,... | collective-permute-start | bytes 589832 | tf_op jit(solution)/shard_map/ppermute | solution.py:64
  197.1 12.4 %collective-permute-start.25 = (bf16[128,384]{1,0:T(8,128)(2,1)S(1)}, bf16[128,384]{1,0:T(8,128)(2,1)S(1)}, u32[]{:S(2)}, u32[]{:S(2)}) collective-permute-start(bf16[128,384]{1,0:T(8,128)(2,1)S(1)} %get-tuple-element.45), channel_id=1, source_target_pairs={{0,0},{4,4},{8,8},{12,12},{16,16},{20,20},{24,24},{28,28},{32,32},... | collective-permute-start | bytes 294920 | tf_op jit(solution)/shard_map/ppermute | solution.py:52
  200.5 12.5 %collective-permute-start.26 = (bf16[128,384]{1,0:T(8,128)(2,1)S(1)}, bf16[128,384]{1,0:T(8,128)(2,1)S(1)}, u32[]{:S(2)}, u32[]{:S(2)}) collective-permute-start(bf16[128,384]{1,0:T(8,128)(2,1)S(1)} %get-tuple-element.46), channel_id=1, source_target_pairs={{4,0},{0,4},{12,8},{8,12},{20,16},{16,20},{28,24},{24,28},{36,32},... | collective-permute-start | bytes 294920 | tf_op jit(solution)/shard_map/ppermute | solution.py:52
  207.2 9.4 %collective-permute-start.10 = (bf16[128,384]{1,0:T(8,128)(2,1)S(1)}, bf16[128,384]{1,0:T(8,128)(2,1)S(1)}, u32[]{:S(2)}, u32[]{:S(2)}) collective-permute-start(bf16[128,384]{1,0:T(8,128)(2,1)S(1)} %get-tuple-element.39), channel_id=1, source_target_pairs={{0,0},{4,4},{8,8},{12,12},{16,16},{20,20},{24,24},{28,28},{32,32},... | collective-permute-start | bytes 294920 | tf_op jit(solution)/shard_map/ppermute | solution.py:52
  209.1 13.9 %collective-permute-start.11 = (bf16[128,384]{1,0:T(8,128)(2,1)S(1)}, bf16[128,384]{1,0:T(8,128)(2,1)S(1)}, u32[]{:S(2)}, u32[]{:S(2)}) collective-permute-start(bf16[128,384]{1,0:T(8,128)(2,1)S(1)} %get-tuple-element.40), channel_id=1, source_target_pairs={{4,0},{0,4},{12,8},{8,12},{20,16},{16,20},{28,24},{24,28},{36,32},... | collective-permute-start | bytes 294920 | tf_op jit(solution)/shard_map/ppermute | solution.py:52
  213.0 13.3 %collective-permute-start.27 = (bf16[2,32,384]{2,1,0:T(8,128)(2,1)S(1)}, bf16[2,32,384]{2,1,0:T(8,128)(2,1)S(1)}, u32[]{:S(2)}, u32[]{:S(2)}) collective-permute-start(bf16[2,32,384]{2,1,0:T(8,128)(2,1)S(1)} %get-tuple-element.42), channel_id=1, source_target_pairs={{0,24},{4,28},{8,0},{12,4},{16,8},{20,12},{24,16},{28,20},{1,25},{... | collective-permute-start | bytes 147464 | tf_op jit(solution)/shard_map/ppermute | solution.py:56
  214.0 12.6 %collective-permute-start.29 = (bf16[2,32,384]{2,1,0:T(8,128)(2,1)S(1)}, bf16[2,32,384]{2,1,0:T(8,128)(2,1)S(1)}, u32[]{:S(2)}, u32[]{:S(2)}) collective-permute-start(bf16[2,32,384]{2,1,0:T(8,128)(2,1)S(1)} %get-tuple-element.43), channel_id=1, source_target_pairs={{0,8},{4,12},{8,16},{12,20},{16,24},{20,28},{24,0},{28,4},{1,9},{5... | collective-permute-start | bytes 147464 | tf_op jit(solution)/shard_map/ppermute | solution.py:56
  216.4 10.2 %collective-permute-start.28 = (bf16[2,32,384]{2,1,0:T(8,128)(2,1)S(1)}, bf16[2,32,384]{2,1,0:T(8,128)(2,1)S(1)}, u32[]{:S(2)}, u32[]{:S(2)}) collective-permute-start(bf16[2,32,384]{2,1,0:T(8,128)(2,1)S(1)} %get-tuple-element.44), channel_id=1, source_target_pairs={{0,16},{4,20},{8,24},{12,28},{16,0},{20,4},{24,8},{28,12},{1,17},{... | collective-permute-start | bytes 147464 | tf_op jit(solution)/shard_map/ppermute | solution.py:56
  223.1 5.4 %collective-permute-start.12 = (bf16[2,32,384]{2,1,0:T(8,128)(2,1)S(1)}, bf16[2,32,384]{2,1,0:T(8,128)(2,1)S(1)}, u32[]{:S(2)}, u32[]{:S(2)}) collective-permute-start(bf16[2,32,384]{2,1,0:T(8,128)(2,1)S(1)} %get-tuple-element.36), channel_id=1, source_target_pairs={{0,24},{4,28},{8,0},{12,4},{16,8},{20,12},{24,16},{28,20},{1,25},{... | collective-permute-start | bytes 147464 | tf_op jit(solution)/shard_map/ppermute | solution.py:56
  224.0 4.5 %collective-permute-start.14 = (bf16[2,32,384]{2,1,0:T(8,128)(2,1)S(1)}, bf16[2,32,384]{2,1,0:T(8,128)(2,1)S(1)}, u32[]{:S(2)}, u32[]{:S(2)}) collective-permute-start(bf16[2,32,384]{2,1,0:T(8,128)(2,1)S(1)} %get-tuple-element.37), channel_id=1, source_target_pairs={{0,8},{4,12},{8,16},{12,20},{16,24},{20,28},{24,0},{28,4},{1,9},{5... | collective-permute-start | bytes 147464 | tf_op jit(solution)/shard_map/ppermute | solution.py:56
  226.4 5.6 %collective-permute-start.13 = (bf16[2,32,384]{2,1,0:T(8,128)(2,1)S(1)}, bf16[2,32,384]{2,1,0:T(8,128)(2,1)S(1)}, u32[]{:S(2)}, u32[]{:S(2)}) collective-permute-start(bf16[2,32,384]{2,1,0:T(8,128)(2,1)S(1)} %get-tuple-element.38), channel_id=1, source_target_pairs={{0,16},{4,20},{8,24},{12,28},{16,0},{20,4},{24,8},{28,12},{1,17},{... | collective-permute-start | bytes 147464 | tf_op jit(solution)/shard_map/ppermute | solution.py:56
Sparse Core Ops, SparseCore 0:
  104.9 41.5 all-gather.1

commit v3 on v2

--- a/solution.py
+++ b/solution.py
@@ -183,7 +183,7 @@
     half, all_rows = columns.shape[1:]
     rows = all_rows // n_chunk
     hidden = units[0].shape[1]
-    tile = 256
+    tile = 512
     return pl.pallas_call(
         functools.partial(grad_kernel, rows, half),
         grid=(hidden // tile,),
@@ -199,7 +199,7 @@
             bytes_accessed=2 * (columns.size + len(units) * rows * hidden + 2 * half * hidden),
             transcendentals=0,
         ),
-        compiler_params=pltpu.CompilerParams(vmem_limit_bytes=40 << 20),
+        compiler_params=pltpu.CompilerParams(vmem_limit_bytes=48 << 20),
     )(where, columns, *units)
 
 

time: 254 us -> 252 us (level)
    unnamed x12 -> x14, local copies, waits for them, and re-layouts: 5.09 us -> 5.09 us
where the time goes in v3:
time: 252 us; the launch traced here: 251 us
  waiting for transfers between devices  119 us (47%)
  starting transfers between devices  78.3 us (31%)
  Pallas kernels  28.3 us (11%)
  between operations  14.6 us (6%)
  local copies, waits for them, and re-layouts  8.29 us (3%)
    ppermute x12, waiting for transfers between devices, shift(): lax.ppermute(block, 'dp', [(i, i + step) for i in range(n_dp) if 0 <= i +...  61.4 us
    ppermute x12, starting transfers between devices, shift(): lax.ppermute(block, 'dp', [(i, i + step) for i in range(n_dp) if 0 <= i +...  41.3 us
    ppermute x6, waiting for transfers between devices, swap(): lax.ppermute(block, ('tensor', 'expert', 'dp'), swap_pairs(flip, back))  31.8 us
    ppermute x6, starting transfers between devices, shift_y(): lax.ppermute(block, 'tensor', [(y * 2 + core, (y + step) % n_y * 2 + core...  15.9 us
    ppermute x9, waiting for transfers between devices, shift_x(): lax.ppermute(block, 'expert', [(x * 2 + zh, (x + step) % n_x * 2 + zh) fo...  14.5 us
    pallas_call x2, Pallas kernels, slot_part(): pl.pallas_call(functools.partial(slot_kernel, rows, half), in_specs=[pl.B...  12.3 us
    ppermute x6, starting transfers between devices, swap(): lax.ppermute(block, ('tensor', 'expert', 'dp'), swap_pairs(flip, back))  12.3 us
    pallas_call x1, Pallas kernels, grad_of(): pl.pallas_call(functools.partial(grad_kernel, rows, half), grid=(hidden /...  11.5 us
  transfers between devices with their start and end apart: 36, of which 16 were waited for; matrix products, arithmetic and copies ran while one was open for 3% of the time, Pallas kernels for 6%

profile of v3, /device:TPU:166, one launch (start us, length us, event | category | flops | bytes accessed | tf_op | source)
XLA Modules:
  0.0 251.5 jit_solution(11981186382298318893)
XLA Ops:
  7.3 1.6 copy-done.1
  8.9 1.6 copy-done.2
  10.5 2.2 shard_map.68
  12.8 2.9 %collective-permute-start.1 = (bf16[256,2048]{1,0:T(8,128)(2,1)S(1)}, bf16[256,2048]{1,0:T(8,128)(2,1)S(1)}, u32[]{:S(2)}, u32[]{:S(2)}) collective-permute-start(bf16[256,2048]{1,0:T(8,128)(2,1)S(1)} %bitcast.166), channel_id=1, source_target_pairs={{1,0},{2,1},{3,2},{5,4},{6,5},{7,6},{9,8},{10,9},{11,10},{13,12},{... | collective-permute-start | bytes 3145736 | tf_op jit(solution)/shard_map/ppermute | solution.py:76
  15.7 2.9 %collective-permute-start = (bf16[256,2048]{1,0:T(8,128)(2,1)S(1)}, bf16[256,2048]{1,0:T(8,128)(2,1)}, u32[]{:S(2)}, u32[]{:S(2)}) collective-permute-start(bf16[256,2048]{1,0:T(8,128)(2,1)S(1)} %bitcast.167), channel_id=1, source_target_pairs={{0,1},{1,2},{2,3},{4,5},{5,6},{6,7},{8,9},{9,10},{10,11},{12,13},{... | collective-permute-start | bytes 3145736 | tf_op jit(solution)/shard_map/ppermute | solution.py:76
  18.6 2.2 shard_map.70
  20.9 3.9 %collective-permute-start.18 = (bf16[256,2048]{1,0:T(8,128)(2,1)S(1)}, bf16[256,2048]{1,0:T(8,128)(2,1)}, u32[]{:S(2)}, u32[]{:S(2)}) collective-permute-start(bf16[256,2048]{1,0:T(8,128)(2,1)S(1)} %bitcast.170), channel_id=1, source_target_pairs={{1,0},{2,1},{3,2},{5,4},{6,5},{7,6},{9,8},{10,9},{11,10},{13,12},{... | collective-permute-start | bytes 3145736 | tf_op jit(solution)/shard_map/ppermute | solution.py:76
  24.8 1.9 collective-permute-start.15
  26.8 0.6 reduce-window.6
  27.4 0.2 slice_reduce_fusion
  27.8 0.4 convolution_convert_fusion
  28.2 0.6 collective-permute-start.30
  28.8 4.1 %collective-permute-done.30 = bf16[2,64,384]{2,1,0:T(8,128)(2,1)S(1)} collective-permute-done((bf16[2,64,384]{2,1,0:T(8,128)(2,1)S(1)}, bf16[2,64,384]{2,1,0:T(8,128)(2,1)S(1)}, u32[]{:S(2)}, u32[]{:S(2)}) %collective-permute-start.30) | collective-permute-done | bytes 98336 | tf_op jit(solution)/shard_map/ppermute | solution.py:56
  32.9 0.8 collective-permute-start.32
  33.8 5.0 %collective-permute-done.32 = bf16[2,64,384]{2,1,0:T(8,128)(2,1)S(1)} collective-permute-done((bf16[2,64,384]{2,1,0:T(8,128)(2,1)S(1)}, bf16[2,64,384]{2,1,0:T(8,128)(2,1)S(1)}, u32[]{:S(2)}, u32[]{:S(2)}) %collective-permute-start.32) | collective-permute-done | bytes 98336 | tf_op jit(solution)/shard_map/ppermute | solution.py:56
  38.7 0.2 collective-permute-start.31
  38.9 23.2 %collective-permute-done.18.refs_4_.refs_11_ = bf16[256,2048]{1,0:T(8,128)(2,1)} collective-permute-done((bf16[256,2048]{1,0:T(8,128)(2,1)S(1)}, bf16[256,2048]{1,0:T(8,128)(2,1)}, u32[]{:S(2)}, u32[]{:S(2)}) %collective-permute-start.18) | collective-permute-done | bytes 1048608 | tf_op jit(solution)/shard_map/ppermute | solution.py:76
  62.1 2.9 %collective-permute-start.19 = (bf16[256,2048]{1,0:T(8,128)(2,1)}, bf16[256,2048]{1,0:T(8,128)(2,1)}, u32[]{:S(2)}, u32[]{:S(2)}) collective-permute-start(bf16[256,2048]{1,0:T(8,128)(2,1)} %collective-permute-done.18.refs_4_.refs_11_), channel_id=1, source_target_pairs={{1,0},{2,1},{3,2},{5,4},{6,5},{7,6},{9,8},{10,9},{11,10},{13,12},{... | collective-permute-start | bytes 3145736 | tf_op jit(solution)/shard_map/ppermute | solution.py:76
  65.1 2.9 %collective-permute-start.16 = (bf16[256,2048]{1,0:T(8,128)(2,1)}, bf16[256,2048]{1,0:T(8,128)(2,1)}, u32[]{:S(2)}, u32[]{:S(2)}) collective-permute-start(bf16[256,2048]{1,0:T(8,128)(2,1)} %collective-permute-done.15.refs_1_.refs_8_), channel_id=1, source_target_pairs={{0,1},{1,2},{2,3},{4,5},{5,6},{6,7},{8,9},{9,10},{10,11},{12,13},{... | collective-permute-start | bytes 3145736 | tf_op jit(solution)/shard_map/ppermute | solution.py:76
  68.1 6.4 %collective-permute-start.33 = (bf16[4,64,384]{2,1,0:T(8,128)(2,1)S(1)}, bf16[4,64,384]{2,1,0:T(8,128)(2,1)S(1)}, u32[]{:S(2)}, u32[]{:S(2)}) collective-permute-start(bf16[4,64,384]{2,1,0:T(8,128)(2,1)S(1)} %get-tuple-element.30), channel_id=1, source_target_pairs={{0,0},{4,4},{8,8},{12,12},{16,16},{20,20},{24,24},{28,28},{32,32},... | collective-permute-start | bytes 589832 | tf_op jit(solution)/shard_map/ppermute | solution.py:52
  74.6 3.6 %collective-permute-start.2 = (bf16[256,2048]{1,0:T(8,128)(2,1)}, bf16[256,2048]{1,0:T(8,128)(2,1)}, u32[]{:S(2)}, u32[]{:S(2)}) collective-permute-start(bf16[256,2048]{1,0:T(8,128)(2,1)} %collective-permute-done.refs_1_), channel_id=1, source_target_pairs={{0,1},{1,2},{2,3},{4,5},{5,6},{6,7},{8,9},{9,10},{10,11},{12,13},{... | collective-permute-start | bytes 3145736 | tf_op jit(solution)/shard_map/ppermute | solution.py:76
  78.2 21.8 %collective-permute-done.33 = bf16[4,64,384]{2,1,0:T(8,128)(2,1)S(1)} collective-permute-done((bf16[4,64,384]{2,1,0:T(8,128)(2,1)S(1)}, bf16[4,64,384]{2,1,0:T(8,128)(2,1)S(1)}, u32[]{:S(2)}, u32[]{:S(2)}) %collective-permute-start.33) | collective-permute-done | bytes 196640 | tf_op jit(solution)/shard_map/ppermute | solution.py:52
  100.0 1.9 collective-permute-start.4
  102.0 0.8 copy.45
  102.8 1.9 copy.46
  104.7 1.9 collective-permute-start.20
  106.7 6.4 %collective-permute-start.17 = (bf16[256,2048]{1,0:T(8,128)(2,1)}, bf16[256,2048]{1,0:T(8,128)(2,1)}, u32[]{:S(2)}, u32[]{:S(2)}) collective-permute-start(bf16[256,2048]{1,0:T(8,128)(2,1)} %collective-permute-done.16.refs_2_.refs_9_), channel_id=1, source_target_pairs={{0,1},{1,2},{2,3},{4,5},{5,6},{6,7},{8,9},{9,10},{10,11},{12,13},{... | collective-permute-start | bytes 3145736 | tf_op jit(solution)/shard_map/ppermute | solution.py:76
  113.1 9.7 %collective-permute-done.2.refs_2_ = bf16[256,2048]{1,0:T(8,128)(2,1)} collective-permute-done((bf16[256,2048]{1,0:T(8,128)(2,1)}, bf16[256,2048]{1,0:T(8,128)(2,1)}, u32[]{:S(2)}, u32[]{:S(2)}) %collective-permute-start.2) | collective-permute-done | bytes 1048608 | tf_op jit(solution)/shard_map/ppermute | solution.py:76
  122.8 8.1 %collective-permute-start.3 = (bf16[256,2048]{1,0:T(8,128)(2,1)}, bf16[256,2048]{1,0:T(8,128)(2,1)}, u32[]{:S(2)}, u32[]{:S(2)}) collective-permute-start(bf16[256,2048]{1,0:T(8,128)(2,1)} %collective-permute-done.2.refs_2_), channel_id=1, source_target_pairs={{0,1},{1,2},{2,3},{4,5},{5,6},{6,7},{8,9},{9,10},{10,11},{12,13},{... | collective-permute-start | bytes 3145736 | tf_op jit(solution)/shard_map/ppermute | solution.py:76
  130.9 1.9 collective-permute-start.5
  132.9 17.6 %collective-permute-done.20.refs_6_.refs_13_ = bf16[256,2048]{1,0:T(8,128)(2,1)} collective-permute-done((bf16[256,2048]{1,0:T(8,128)(2,1)}, bf16[256,2048]{1,0:T(8,128)(2,1)}, u32[]{:S(2)}, u32[]{:S(2)}) %collective-permute-start.20) | collective-permute-done | bytes 1048608 | tf_op jit(solution)/shard_map/ppermute | solution.py:76
  150.6 1.9 copy-done.4
  152.5 6.0 %shard_map.71 = (bf16[4,256,384]{2,1,0:T(8,128)(2,1)S(1)}, bf16[4,256,384]{2,1,0:T(8,128)(2,1)S(1)}) custom-call(s32[3]{0:T(128)S(1)} %pad_add_fusion.where_ref, bf16[256,2048]{1,0:T(8,128)(2,1)S(1)} %bitcast.172, bf16[256,2048]{1,0:T(8,128)(2,1)} %collective-permute-done.15.refs_1_.refs_8_, bf16[256,2048]{1,0:T(8,128)(2,1)} %collective-permute-done.16.refs_2_.refs_9_, ...), custom_call_target="tpu_custom_call" | custom-call | flops 3221225472 | bytes 7340032 | tf_op jit(solution)/shard_map/pallas_call | solution.py:143
  158.6 6.8 %collective-permute-done.3.refs_3_ = bf16[256,2048]{1,0:T(8,128)(2,1)} collective-permute-done((bf16[256,2048]{1,0:T(8,128)(2,1)}, bf16[256,2048]{1,0:T(8,128)(2,1)}, u32[]{:S(2)}, u32[]{:S(2)}) %collective-permute-start.3) | collective-permute-done | bytes 1048608 | tf_op jit(solution)/shard_map/ppermute | solution.py:76
  165.4 4.1 %collective-permute-done.5.refs_6_ = bf16[256,2048]{1,0:T(8,128)(2,1)} collective-permute-done((bf16[256,2048]{1,0:T(8,128)(2,1)}, bf16[256,2048]{1,0:T(8,128)(2,1)}, u32[]{:S(2)}, u32[]{:S(2)}) %collective-permute-start.5) | collective-permute-done | bytes 1048608 | tf_op jit(solution)/shard_map/ppermute | solution.py:76
  169.5 6.2 %shard_map.69 = (bf16[4,256,384]{2,1,0:T(8,128)(2,1)S(1)}, bf16[4,256,384]{2,1,0:T(8,128)(2,1)S(1)}) custom-call(s32[3]{0:T(128)S(1)} %pad_add_fusion.where_ref, bf16[256,2048]{1,0:T(8,128)(2,1)S(1)} %bitcast.168, bf16[256,2048]{1,0:T(8,128)(2,1)} %collective-permute-done.refs_1_, bf16[256,2048]{1,0:T(8,128)(2,1)} %collective-permute-done.2.refs_2_, ...), custom_call_target="tpu_custom_call" | custom-call | flops 3221225472 | bytes 7340032 | tf_op jit(solution)/shard_map/pallas_call | solution.py:143
  175.8 0.2 fusion.45
  176.1 8.8 %collective-permute-start.22 = (bf16[256,384]{1,0:T(8,128)(2,1)S(1)}, bf16[256,384]{1,0:T(8,128)(2,1)S(1)}, u32[]{:S(2)}, u32[]{:S(2)}) collective-permute-start(bf16[256,384]{1,0:T(8,128)(2,1)S(1)} %get-tuple-element.27), channel_id=1, source_target_pairs={{0,64},{32,96},{64,128},{96,160},{128,192},{160,224},{192,0},{224,... | collective-permute-start | bytes 589832 | tf_op jit(solution)/shard_map/ppermute | solution.py:64
  184.9 0.8 collective-permute-start.24
  185.7 1.4 collective-permute-start.23
  187.1 0.2 fusion.44
  187.4 1.5 collective-permute-start.7
  188.9 1.8 collective-permute-start.9
  190.7 0.4 collective-permute-done.22
  191.1 1.6 collective-permute-start.8
  192.7 4.2 %collective-permute-done.23 = bf16[256,384]{1,0:T(8,128)(2,1)S(1)} collective-permute-done((bf16[256,384]{1,0:T(8,128)(2,1)S(1)}, bf16[256,384]{1,0:T(8,128)(2,1)S(1)}, u32[]{:S(2)}, u32[]{:S(2)}) %collective-permute-start.23) | collective-permute-done | bytes 196640 | tf_op jit(solution)/shard_map/ppermute | solution.py:64
  197.1 3.4 %collective-permute-start.25 = (bf16[128,384]{1,0:T(8,128)(2,1)S(1)}, bf16[128,384]{1,0:T(8,128)(2,1)S(1)}, u32[]{:S(2)}, u32[]{:S(2)}) collective-permute-start(bf16[128,384]{1,0:T(8,128)(2,1)S(1)} %get-tuple-element.45), channel_id=1, source_target_pairs={{0,0},{4,4},{8,8},{12,12},{16,16},{20,20},{24,24},{28,28},{32,32},... | collective-permute-start | bytes 294920 | tf_op jit(solution)/shard_map/ppermute | solution.py:52
  200.6 0.5 collective-permute-done.9
  201.1 5.9 %collective-permute-done.8 = bf16[256,384]{1,0:T(8,128)(2,1)S(1)} collective-permute-done((bf16[256,384]{1,0:T(8,128)(2,1)S(1)}, bf16[256,384]{1,0:T(8,128)(2,1)S(1)}, u32[]{:S(2)}, u32[]{:S(2)}) %collective-permute-start.8) | collective-permute-done | bytes 196640 | tf_op jit(solution)/shard_map/ppermute | solution.py:64
  207.2 1.9 collective-permute-start.10
  209.1 0.4 collective-permute-start.11
  209.5 3.5 %collective-permute-done.26 = bf16[128,384]{1,0:T(8,128)(2,1)S(1)} collective-permute-done((bf16[128,384]{1,0:T(8,128)(2,1)S(1)}, bf16[128,384]{1,0:T(8,128)(2,1)S(1)}, u32[]{:S(2)}, u32[]{:S(2)}) %collective-permute-start.26) | collective-permute-done | bytes 98336 | tf_op jit(solution)/shard_map/ppermute | solution.py:52
  213.0 0.9 collective-permute-start.27
  214.0 2.4 collective-permute-start.29
  216.4 0.2 collective-permute-start.28
  216.6 6.5 %collective-permute-done.11 = bf16[128,384]{1,0:T(8,128)(2,1)S(1)} collective-permute-done((bf16[128,384]{1,0:T(8,128)(2,1)S(1)}, bf16[128,384]{1,0:T(8,128)(2,1)S(1)}, u32[]{:S(2)}, u32[]{:S(2)}) %collective-permute-start.11) | collective-permute-done | bytes 98336 | tf_op jit(solution)/shard_map/ppermute | solution.py:52
  223.1 0.9 collective-permute-start.12
  224.0 2.4 collective-permute-start.14
  226.4 0.2 collective-permute-start.13
  226.6 1.8 collective-permute-done.12
  228.4 3.5 %collective-permute-done.13 = bf16[2,32,384]{2,1,0:T(8,128)(2,1)S(1)} collective-permute-done((bf16[2,32,384]{2,1,0:T(8,128)(2,1)S(1)}, bf16[2,32,384]{2,1,0:T(8,128)(2,1)S(1)}, u32[]{:S(2)}, u32[]{:S(2)}) %collective-permute-start.13) | collective-permute-done | bytes 49184 | tf_op jit(solution)/shard_map/ppermute | solution.py:56
  232.0 0.2 fusion.16
  232.2 0.9 fusion
  233.1 11.5 %shard_map.72 = bf16[768,2048]{1,0:T(8,128)(2,1)} custom-call(s32[3]{0:T(128)S(1)} %pad_add_fusion.where_ref, bf16[8,384,512]{2,1,0:T(8,128)(2,1)} %all-gather.2.cloned.1.call-done.x_ref, bf16[256,2048]{1,0:T(8,128)(2,1)S(1)} %bitcast.169, bf16[256,2048]{1,0:T(8,128)(2,1)} %collective-permute-done.refs_1_, bf16[256,2048]{1,0:T(8,128)(2,1)} %collective-permute-done.2.refs_2_, ...), custom_call_target="tpu_custom_call" | custom-call | flops 6442450944 | bytes 20971520 | tf_op jit(solution)/shard_map/pallas_call | solution.py:187
  (63 shorter events, 1.5 us)
Async XLA Ops:
  7.2 20.6 %copy-start = (bf16[128,384]{1,0:T(8,128)(2,1)S(1)}, bf16[128,384]{1,0:T(8,128)(2,1)}, u32[]{:S(2)}) copy-start(bf16[128,384]{1,0:T(8,128)(2,1)} %param.5) | copy-start | bytes 294916
  7.2 225.9 %all-gather.2.cloned.1.call-start = ((), (), s32[]{:S(2)}) async-start(), calls=%async_computation | async-start | bytes 3538944 | tf_op jit(solution)/shard_map/all_gather | solution.py:246
  7.3 1.6 copy-start.1
  8.9 1.6 copy-start.2
  12.8 14.0 %copy-start.6 = (s32[128,2]{0,1:T(2,128)S(1)}, s32[128,2]{0,1:T(2,128)}, u32[]{:S(2)}) copy-start(s32[128,2]{0,1:T(2,128)} %param.6) | copy-start | bytes 3076
  12.8 61.7 %collective-permute-start.1 = (bf16[256,2048]{1,0:T(8,128)(2,1)S(1)}, bf16[256,2048]{1,0:T(8,128)(2,1)S(1)}, u32[]{:S(2)}, u32[]{:S(2)}) collective-permute-start(bf16[256,2048]{1,0:T(8,128)(2,1)S(1)} %bitcast.166), channel_id=1, source_target_pairs={{1,0},{2,1},{3,2},{5,4},{6,5},{7,6},{9,8},{10,9},{11,10},{13,12},{... | collective-permute-start | bytes 3145736 | tf_op jit(solution)/shard_map/ppermute | solution.py:76
  15.7 58.9 %collective-permute-start = (bf16[256,2048]{1,0:T(8,128)(2,1)S(1)}, bf16[256,2048]{1,0:T(8,128)(2,1)}, u32[]{:S(2)}, u32[]{:S(2)}) collective-permute-start(bf16[256,2048]{1,0:T(8,128)(2,1)S(1)} %bitcast.167), channel_id=1, source_target_pairs={{0,1},{1,2},{2,3},{4,5},{5,6},{6,7},{8,9},{9,10},{10,11},{12,13},{... | collective-permute-start | bytes 3145736 | tf_op jit(solution)/shard_map/ppermute | solution.py:76
  20.9 129.7 %copy-start.3 = (bf16[2,4,32,2048]{3,2,1,0:T(8,128)(2,1)}, bf16[2,4,32,2048]{3,2,1,0:T(8,128)(2,1)S(1)}, u32[]{:S(2)}) copy-start(bf16[2,4,32,2048]{3,2,1,0:T(8,128)(2,1)S(1)} %shard_map.70) | copy-start | bytes 3145732
  20.9 41.2 %collective-permute-start.18 = (bf16[256,2048]{1,0:T(8,128)(2,1)S(1)}, bf16[256,2048]{1,0:T(8,128)(2,1)}, u32[]{:S(2)}, u32[]{:S(2)}) collective-permute-start(bf16[256,2048]{1,0:T(8,128)(2,1)S(1)} %bitcast.170), channel_id=1, source_target_pairs={{1,0},{2,1},{3,2},{5,4},{6,5},{7,6},{9,8},{10,9},{11,10},{13,12},{... | collective-permute-start | bytes 3145736 | tf_op jit(solution)/shard_map/ppermute | solution.py:76
  24.8 40.2 %collective-permute-start.15 = (bf16[256,2048]{1,0:T(8,128)(2,1)S(1)}, bf16[256,2048]{1,0:T(8,128)(2,1)}, u32[]{:S(2)}, u32[]{:S(2)}) collective-permute-start(bf16[256,2048]{1,0:T(8,128)(2,1)S(1)} %bitcast.171), channel_id=1, source_target_pairs={{0,1},{1,2},{2,3},{4,5},{5,6},{6,7},{8,9},{9,10},{10,11},{12,13},{... | collective-permute-start | bytes 3145736 | tf_op jit(solution)/shard_map/ppermute | solution.py:76
  28.2 4.7 %collective-permute-start.30 = (bf16[2,64,384]{2,1,0:T(8,128)(2,1)S(1)}, bf16[2,64,384]{2,1,0:T(8,128)(2,1)S(1)}, u32[]{:S(2)}, u32[]{:S(2)}) collective-permute-start(bf16[2,64,384]{2,1,0:T(8,128)(2,1)S(1)} %get-tuple-element.32), channel_id=1, source_target_pairs={{0,8},{4,12},{8,16},{12,20},{16,24},{20,28},{24,0},{28,4},{1,9},{5... | collective-permute-start | bytes 294920 | tf_op jit(solution)/shard_map/ppermute | solution.py:56
  32.9 5.8 %collective-permute-start.32 = (bf16[2,64,384]{2,1,0:T(8,128)(2,1)S(1)}, bf16[2,64,384]{2,1,0:T(8,128)(2,1)S(1)}, u32[]{:S(2)}, u32[]{:S(2)}) collective-permute-start(bf16[2,64,384]{2,1,0:T(8,128)(2,1)S(1)} %get-tuple-element.33), channel_id=1, source_target_pairs={{0,24},{4,28},{8,0},{12,4},{16,8},{20,12},{24,16},{28,20},{1,25},{... | collective-permute-start | bytes 294920 | tf_op jit(solution)/shard_map/ppermute | solution.py:56
  38.7 29.3 %collective-permute-start.31 = (bf16[2,64,384]{2,1,0:T(8,128)(2,1)S(1)}, bf16[2,64,384]{2,1,0:T(8,128)(2,1)S(1)}, u32[]{:S(2)}, u32[]{:S(2)}) collective-permute-start(bf16[2,64,384]{2,1,0:T(8,128)(2,1)S(1)} %get-tuple-element.34), channel_id=1, source_target_pairs={{0,16},{4,20},{8,24},{12,28},{16,0},{20,4},{24,8},{28,12},{1,17},{... | collective-permute-start | bytes 294920 | tf_op jit(solution)/shard_map/ppermute | solution.py:56
  62.1 42.6 %collective-permute-start.19 = (bf16[256,2048]{1,0:T(8,128)(2,1)}, bf16[256,2048]{1,0:T(8,128)(2,1)}, u32[]{:S(2)}, u32[]{:S(2)}) collective-permute-start(bf16[256,2048]{1,0:T(8,128)(2,1)} %collective-permute-done.18.refs_4_.refs_11_), channel_id=1, source_target_pairs={{1,0},{2,1},{3,2},{5,4},{6,5},{7,6},{9,8},{10,9},{11,10},{13,12},{... | collective-permute-start | bytes 3145736 | tf_op jit(solution)/shard_map/ppermute | solution.py:76
  65.1 41.6 %collective-permute-start.16 = (bf16[256,2048]{1,0:T(8,128)(2,1)}, bf16[256,2048]{1,0:T(8,128)(2,1)}, u32[]{:S(2)}, u32[]{:S(2)}) collective-permute-start(bf16[256,2048]{1,0:T(8,128)(2,1)} %collective-permute-done.15.refs_1_.refs_8_), channel_id=1, source_target_pairs={{0,1},{1,2},{2,3},{4,5},{5,6},{6,7},{8,9},{9,10},{10,11},{12,13},{... | collective-permute-start | bytes 3145736 | tf_op jit(solution)/shard_map/ppermute | solution.py:76
  68.1 31.9 %collective-permute-start.33 = (bf16[4,64,384]{2,1,0:T(8,128)(2,1)S(1)}, bf16[4,64,384]{2,1,0:T(8,128)(2,1)S(1)}, u32[]{:S(2)}, u32[]{:S(2)}) collective-permute-start(bf16[4,64,384]{2,1,0:T(8,128)(2,1)S(1)} %get-tuple-element.30), channel_id=1, source_target_pairs={{0,0},{4,4},{8,8},{12,12},{16,16},{20,20},{24,24},{28,28},{32,32},... | collective-permute-start | bytes 589832 | tf_op jit(solution)/shard_map/ppermute | solution.py:52
  74.5 27.4 %collective-permute-start.34 = (bf16[4,64,384]{2,1,0:T(8,128)(2,1)S(1)}, bf16[4,64,384]{2,1,0:T(8,128)(2,1)S(1)}, u32[]{:S(2)}, u32[]{:S(2)}) collective-permute-start(bf16[4,64,384]{2,1,0:T(8,128)(2,1)S(1)} %get-tuple-element.31), channel_id=1, source_target_pairs={{0,4},{4,0},{8,12},{12,8},{16,20},{20,16},{24,28},{28,24},{32,36},... | collective-permute-start | bytes 589832 | tf_op jit(solution)/shard_map/ppermute | solution.py:52
  74.6 48.2 %collective-permute-start.2 = (bf16[256,2048]{1,0:T(8,128)(2,1)}, bf16[256,2048]{1,0:T(8,128)(2,1)}, u32[]{:S(2)}, u32[]{:S(2)}) collective-permute-start(bf16[256,2048]{1,0:T(8,128)(2,1)} %collective-permute-done.refs_1_), channel_id=1, source_target_pairs={{0,1},{1,2},{2,3},{4,5},{5,6},{6,7},{8,9},{9,10},{10,11},{12,13},{... | collective-permute-start | bytes 3145736 | tf_op jit(solution)/shard_map/ppermute | solution.py:76
  100.0 30.9 %collective-permute-start.4 = (bf16[256,2048]{1,0:T(8,128)(2,1)S(1)}, bf16[256,2048]{1,0:T(8,128)(2,1)}, u32[]{:S(2)}, u32[]{:S(2)}) collective-permute-start(bf16[256,2048]{1,0:T(8,128)(2,1)S(1)} %collective-permute-done.1.refs_4_), channel_id=1, source_target_pairs={{1,0},{2,1},{3,2},{5,4},{6,5},{7,6},{9,8},{10,9},{11,10},{13,12},{... | collective-permute-start | bytes 3145736 | tf_op jit(solution)/shard_map/ppermute | solution.py:76
  104.7 45.8 %collective-permute-start.20 = (bf16[256,2048]{1,0:T(8,128)(2,1)}, bf16[256,2048]{1,0:T(8,128)(2,1)}, u32[]{:S(2)}, u32[]{:S(2)}) collective-permute-start(bf16[256,2048]{1,0:T(8,128)(2,1)} %collective-permute-done.19.refs_5_.refs_12_), channel_id=1, source_target_pairs={{1,0},{2,1},{3,2},{5,4},{6,5},{7,6},{9,8},{10,9},{11,10},{13,12},{... | collective-permute-start | bytes 3145736 | tf_op jit(solution)/shard_map/ppermute | solution.py:76
  106.7 43.9 %collective-permute-start.17 = (bf16[256,2048]{1,0:T(8,128)(2,1)}, bf16[256,2048]{1,0:T(8,128)(2,1)}, u32[]{:S(2)}, u32[]{:S(2)}) collective-permute-start(bf16[256,2048]{1,0:T(8,128)(2,1)} %collective-permute-done.16.refs_2_.refs_9_), channel_id=1, source_target_pairs={{0,1},{1,2},{2,3},{4,5},{5,6},{6,7},{8,9},{9,10},{10,11},{12,13},{... | collective-permute-start | bytes 3145736 | tf_op jit(solution)/shard_map/ppermute | solution.py:76
  122.8 42.6 %collective-permute-start.3 = (bf16[256,2048]{1,0:T(8,128)(2,1)}, bf16[256,2048]{1,0:T(8,128)(2,1)}, u32[]{:S(2)}, u32[]{:S(2)}) collective-permute-start(bf16[256,2048]{1,0:T(8,128)(2,1)} %collective-permute-done.2.refs_2_), channel_id=1, source_target_pairs={{0,1},{1,2},{2,3},{4,5},{5,6},{6,7},{8,9},{9,10},{10,11},{12,13},{... | collective-permute-start | bytes 3145736 | tf_op jit(solution)/shard_map/ppermute | solution.py:76
  130.9 38.5 %collective-permute-start.5 = (bf16[256,2048]{1,0:T(8,128)(2,1)}, bf16[256,2048]{1,0:T(8,128)(2,1)}, u32[]{:S(2)}, u32[]{:S(2)}) collective-permute-start(bf16[256,2048]{1,0:T(8,128)(2,1)} %collective-permute-done.4.refs_5_), channel_id=1, source_target_pairs={{1,0},{2,1},{3,2},{5,4},{6,5},{7,6},{9,8},{10,9},{11,10},{13,12},{... | collective-permute-start | bytes 3145736 | tf_op jit(solution)/shard_map/ppermute | solution.py:76
  150.6 1.9 copy-start.4
  152.5 17.0 %copy-start.5 = (bf16[1,768,2048]{2,1,0:T(8,128)(2,1)S(1)}, bf16[1,768,2048]{2,1,0:T(8,128)(2,1)}, u32[]{:S(2)}) copy-start(bf16[1,768,2048]{2,1,0:T(8,128)(2,1)} %param.7) | copy-start | bytes 9437188
  158.5 17.3 %collective-permute-start.21 = (bf16[4,256,384]{2,1,0:T(8,128)(2,1)S(1)}, bf16[4,256,384]{2,1,0:T(8,128)(2,1)S(1)}, u32[]{:S(2)}, u32[]{:S(2)}) collective-permute-start(bf16[4,256,384]{2,1,0:T(8,128)(2,1)S(1)} %get-tuple-element.16), channel_id=1, source_target_pairs={{0,32},{32,0},{64,96},{96,64},{128,160},{160,128},{192,224},{224,1... | collective-permute-start | bytes 2359304 | tf_op jit(solution)/shard_map/ppermute | solution.py:72
  175.7 11.4 %collective-permute-start.6 = (bf16[4,256,384]{2,1,0:T(8,128)(2,1)S(1)}, bf16[4,256,384]{2,1,0:T(8,128)(2,1)S(1)}, u32[]{:S(2)}, u32[]{:S(2)}) collective-permute-start(bf16[4,256,384]{2,1,0:T(8,128)(2,1)S(1)} %get-tuple-element.14), channel_id=1, source_target_pairs={{0,32},{32,0},{64,96},{96,64},{128,160},{160,128},{192,224},{224,1... | collective-permute-start | bytes 2359304 | tf_op jit(solution)/shard_map/ppermute | solution.py:72
  176.1 15.0 %collective-permute-start.22 = (bf16[256,384]{1,0:T(8,128)(2,1)S(1)}, bf16[256,384]{1,0:T(8,128)(2,1)S(1)}, u32[]{:S(2)}, u32[]{:S(2)}) collective-permute-start(bf16[256,384]{1,0:T(8,128)(2,1)S(1)} %get-tuple-element.27), channel_id=1, source_target_pairs={{0,64},{32,96},{64,128},{96,160},{128,192},{160,224},{192,0},{224,... | collective-permute-start | bytes 589832 | tf_op jit(solution)/shard_map/ppermute | solution.py:64
  184.9 7.8 %collective-permute-start.24 = (bf16[256,384]{1,0:T(8,128)(2,1)S(1)}, bf16[256,384]{1,0:T(8,128)(2,1)S(1)}, u32[]{:S(2)}, u32[]{:S(2)}) collective-permute-start(bf16[256,384]{1,0:T(8,128)(2,1)S(1)} %get-tuple-element.28), channel_id=1, source_target_pairs={{0,192},{32,224},{64,0},{96,32},{128,64},{160,96},{192,128},{224,1... | collective-permute-start | bytes 589832 | tf_op jit(solution)/shard_map/ppermute | solution.py:64
  185.7 11.3 %collective-permute-start.23 = (bf16[256,384]{1,0:T(8,128)(2,1)S(1)}, bf16[256,384]{1,0:T(8,128)(2,1)S(1)}, u32[]{:S(2)}, u32[]{:S(2)}) collective-permute-start(bf16[256,384]{1,0:T(8,128)(2,1)S(1)} %get-tuple-element.29), channel_id=1, source_target_pairs={{0,128},{32,160},{64,192},{96,224},{128,0},{160,32},{192,64},{224,... | collective-permute-start | bytes 589832 | tf_op jit(solution)/shard_map/ppermute | solution.py:64
  187.4 13.2 %collective-permute-start.7 = (bf16[256,384]{1,0:T(8,128)(2,1)S(1)}, bf16[256,384]{1,0:T(8,128)(2,1)S(1)}, u32[]{:S(2)}, u32[]{:S(2)}) collective-permute-start(bf16[256,384]{1,0:T(8,128)(2,1)S(1)} %get-tuple-element.24), channel_id=1, source_target_pairs={{0,64},{32,96},{64,128},{96,160},{128,192},{160,224},{192,0},{224,... | collective-permute-start | bytes 589832 | tf_op jit(solution)/shard_map/ppermute | solution.py:64
  188.9 12.3 %collective-permute-start.9 = (bf16[256,384]{1,0:T(8,128)(2,1)S(1)}, bf16[256,384]{1,0:T(8,128)(2,1)S(1)}, u32[]{:S(2)}, u32[]{:S(2)}) collective-permute-start(bf16[256,384]{1,0:T(8,128)(2,1)S(1)} %get-tuple-element.25), channel_id=1, source_target_pairs={{0,192},{32,224},{64,0},{96,32},{128,64},{160,96},{192,128},{224,1... | collective-permute-start | bytes 589832 | tf_op jit(solution)/shard_map/ppermute | solution.py:64
  191.1 15.9 %collective-permute-start.8 = (bf16[256,384]{1,0:T(8,128)(2,1)S(1)}, bf16[256,384]{1,0:T(8,128)(2,1)S(1)}, u32[]{:S(2)}, u32[]{:S(2)}) collective-permute-start(bf16[256,384]{1,0:T(8,128)(2,1)S(1)} %get-tuple-element.26), channel_id=1, source_target_pairs={{0,128},{32,160},{64,192},{96,224},{128,0},{160,32},{192,64},{224,... | collective-permute-start | bytes 589832 | tf_op jit(solution)/shard_map/ppermute | solution.py:64
  197.1 12.4 %collective-permute-start.25 = (bf16[128,384]{1,0:T(8,128)(2,1)S(1)}, bf16[128,384]{1,0:T(8,128)(2,1)S(1)}, u32[]{:S(2)}, u32[]{:S(2)}) collective-permute-start(bf16[128,384]{1,0:T(8,128)(2,1)S(1)} %get-tuple-element.45), channel_id=1, source_target_pairs={{0,0},{4,4},{8,8},{12,12},{16,16},{20,20},{24,24},{28,28},{32,32},... | collective-permute-start | bytes 294920 | tf_op jit(solution)/shard_map/ppermute | solution.py:52
  200.5 12.5 %collective-permute-start.26 = (bf16[128,384]{1,0:T(8,128)(2,1)S(1)}, bf16[128,384]{1,0:T(8,128)(2,1)S(1)}, u32[]{:S(2)}, u32[]{:S(2)}) collective-permute-start(bf16[128,384]{1,0:T(8,128)(2,1)S(1)} %get-tuple-element.46), channel_id=1, source_target_pairs={{4,0},{0,4},{12,8},{8,12},{20,16},{16,20},{28,24},{24,28},{36,32},... | collective-permute-start | bytes 294920 | tf_op jit(solution)/shard_map/ppermute | solution.py:52
  207.2 9.4 %collective-permute-start.10 = (bf16[128,384]{1,0:T(8,128)(2,1)S(1)}, bf16[128,384]{1,0:T(8,128)(2,1)S(1)}, u32[]{:S(2)}, u32[]{:S(2)}) collective-permute-start(bf16[128,384]{1,0:T(8,128)(2,1)S(1)} %get-tuple-element.39), channel_id=1, source_target_pairs={{0,0},{4,4},{8,8},{12,12},{16,16},{20,20},{24,24},{28,28},{32,32},... | collective-permute-start | bytes 294920 | tf_op jit(solution)/shard_map/ppermute | solution.py:52
  209.1 13.9 %collective-permute-start.11 = (bf16[128,384]{1,0:T(8,128)(2,1)S(1)}, bf16[128,384]{1,0:T(8,128)(2,1)S(1)}, u32[]{:S(2)}, u32[]{:S(2)}) collective-permute-start(bf16[128,384]{1,0:T(8,128)(2,1)S(1)} %get-tuple-element.40), channel_id=1, source_target_pairs={{4,0},{0,4},{12,8},{8,12},{20,16},{16,20},{28,24},{24,28},{36,32},... | collective-permute-start | bytes 294920 | tf_op jit(solution)/shard_map/ppermute | solution.py:52
  213.0 13.3 %collective-permute-start.27 = (bf16[2,32,384]{2,1,0:T(8,128)(2,1)S(1)}, bf16[2,32,384]{2,1,0:T(8,128)(2,1)S(1)}, u32[]{:S(2)}, u32[]{:S(2)}) collective-permute-start(bf16[2,32,384]{2,1,0:T(8,128)(2,1)S(1)} %get-tuple-element.42), channel_id=1, source_target_pairs={{0,24},{4,28},{8,0},{12,4},{16,8},{20,12},{24,16},{28,20},{1,25},{... | collective-permute-start | bytes 147464 | tf_op jit(solution)/shard_map/ppermute | solution.py:56
  214.0 12.6 %collective-permute-start.29 = (bf16[2,32,384]{2,1,0:T(8,128)(2,1)S(1)}, bf16[2,32,384]{2,1,0:T(8,128)(2,1)S(1)}, u32[]{:S(2)}, u32[]{:S(2)}) collective-permute-start(bf16[2,32,384]{2,1,0:T(8,128)(2,1)S(1)} %get-tuple-element.43), channel_id=1, source_target_pairs={{0,8},{4,12},{8,16},{12,20},{16,24},{20,28},{24,0},{28,4},{1,9},{5... | collective-permute-start | bytes 147464 | tf_op jit(solution)/shard_map/ppermute | solution.py:56
  216.4 10.2 %collective-permute-start.28 = (bf16[2,32,384]{2,1,0:T(8,128)(2,1)S(1)}, bf16[2,32,384]{2,1,0:T(8,128)(2,1)S(1)}, u32[]{:S(2)}, u32[]{:S(2)}) collective-permute-start(bf16[2,32,384]{2,1,0:T(8,128)(2,1)S(1)} %get-tuple-element.44), channel_id=1, source_target_pairs={{0,16},{4,20},{8,24},{12,28},{16,0},{20,4},{24,8},{28,12},{1,17},{... | collective-permute-start | bytes 147464 | tf_op jit(solution)/shard_map/ppermute | solution.py:56
  223.1 5.4 %collective-permute-start.12 = (bf16[2,32,384]{2,1,0:T(8,128)(2,1)S(1)}, bf16[2,32,384]{2,1,0:T(8,128)(2,1)S(1)}, u32[]{:S(2)}, u32[]{:S(2)}) collective-permute-start(bf16[2,32,384]{2,1,0:T(8,128)(2,1)S(1)} %get-tuple-element.36), channel_id=1, source_target_pairs={{0,24},{4,28},{8,0},{12,4},{16,8},{20,12},{24,16},{28,20},{1,25},{... | collective-permute-start | bytes 147464 | tf_op jit(solution)/shard_map/ppermute | solution.py:56
  224.0 4.5 %collective-permute-start.14 = (bf16[2,32,384]{2,1,0:T(8,128)(2,1)S(1)}, bf16[2,32,384]{2,1,0:T(8,128)(2,1)S(1)}, u32[]{:S(2)}, u32[]{:S(2)}) collective-permute-start(bf16[2,32,384]{2,1,0:T(8,128)(2,1)S(1)} %get-tuple-element.37), channel_id=1, source_target_pairs={{0,8},{4,12},{8,16},{12,20},{16,24},{20,28},{24,0},{28,4},{1,9},{5... | collective-permute-start | bytes 147464 | tf_op jit(solution)/shard_map/ppermute | solution.py:56
  226.4 5.6 %collective-permute-start.13 = (bf16[2,32,384]{2,1,0:T(8,128)(2,1)S(1)}, bf16[2,32,384]{2,1,0:T(8,128)(2,1)S(1)}, u32[]{:S(2)}, u32[]{:S(2)}) collective-permute-start(bf16[2,32,384]{2,1,0:T(8,128)(2,1)S(1)} %get-tuple-element.38), channel_id=1, source_target_pairs={{0,16},{4,20},{8,24},{12,28},{16,0},{20,4},{24,8},{28,12},{1,17},{... | collective-permute-start | bytes 147464 | tf_op jit(solution)/shard_map/ppermute | solution.py:56
Sparse Core Ops, SparseCore 0:
  104.9 41.5 all-gather.1
